TPU v7x, 32 devices: a whole 2x2x4 slice. The times are simulated.
32 devices in a mesh: own: 4 (over z), img: 8 (over y, x, core).
Axes of the slice: x: 2, y: 2, z: 4, core: 2. Of those that a mesh axis runs over, the one named last changes fastest.
Arguments:
- mask_field: bfloat16 [4096, 4096], P('own', 'img'), may hold values from -1 to 1
- target_field: bfloat16 [4096, 4096], P('own', 'img'), may hold values from 0 to 1
- occupancy: int32 [8, 8], replicated, may hold values 0 or 1
- kernels: float32 [2, 24, 32, 32], replicated, may hold values from -9 to 9
- weights: float32 [24], replicated, may hold values from 0.01 to 0.3
Outputs:
- gradient: float32 [4096, 4096], P('own', 'img')
All inputs are finite; a program needn't handle non-finite values.
Results may differ from a plain program's by a relative error of at most 0.0072.
Values may be sent and summed in bfloat16 or wider, within the bound.
A program may use at most 64 MiB of HBM per device.

v0:
```python
import math

import jax
import jax.numpy as jnp
import numpy as np
from jax import lax
from jax.experimental import pallas as pl
from jax.experimental.pallas import tpu as pltpu
from jax.sharding import PartitionSpec as P

TILE = 512
AMBIT = 64
FREQ = 32
KERNELS = 24
PAD = 640
STEEP = 2.0
THRESHOLD = 1.5
GAMMA = 0.25
GROUP = 8
BH = 256
BW = 128
BATCH = 4


def tables():
    freqs = np.arange(FREQ) - FREQ // 2
    turn = np.float32(2.0 * math.pi / PAD)
    phase = ((freqs[:, None] * np.arange(PAD)[None, :]) % PAD).astype(np.float32) * turn
    back = (((np.arange(TILE) + AMBIT)[:, None] * freqs[None, :]) % PAD).astype(np.float32) * turn
    bf = lambda a: np.asarray(a, np.float32).astype(jnp.bfloat16)
    return (
        bf(np.cos(phase) / np.float32(math.sqrt(PAD))),
        bf(-np.sin(phase) / np.float32(math.sqrt(PAD))),
        bf(np.cos(back) / np.float32(math.sqrt(FREQ))),
        bf(np.sin(back) / np.float32(math.sqrt(FREQ))),
    )


FC, FS, HC, HS = tables()
FORWARD = np.concatenate([FC, FS], 0)
INVERSE = np.concatenate([HC, HS], 1)


def spread(count):
    length = count * TILE
    out = np.zeros((count + 2, 2 * FREQ, length), jnp.bfloat16)
    for tile in range(-1, count + 1):
        start = tile * TILE - AMBIT
        low, high = max(start, 0), min(start + PAD, length)
        out[tile + 1, :, low:high] = FORWARD[:, low - start : high - start]
    return out.reshape(-1, length)


def column_tables():
    there, back = [], []
    for block in range(TILE // BW):
        c = HC[block * BW : (block + 1) * BW].astype(np.float32)
        s = HS[block * BW : (block + 1) * BW].astype(np.float32)
        one = np.block([[c.T, s.T], [-s.T, c.T]])
        there.append(np.concatenate([one, one], 0))
        adj = np.concatenate([np.block([[c, -s], [s, c]]), np.block([[-s, -c], [c, -s]])], 1)
        back.append(np.concatenate([adj, adj], 0))
    return np.stack(there).astype(jnp.bfloat16), np.stack(back).astype(jnp.bfloat16)


THERE, BACK = column_tables()


def mixed_dot(left, right):
    return jnp.dot(left, right, preferred_element_type=jnp.float32)


def two_parts(value):
    high = value.astype(jnp.bfloat16)
    return high, (value - high.astype(jnp.float32)).astype(jnp.bfloat16)


def imaging(slots, occ_ref, spec_ref, targ_ref, kr_ref, ki_ref, h_ref, ht_ref, b_ref, g_ref, out_ref, p_ref, e_ref):
    wide = BATCH * 2 * BW

    def tile(item, carry):
        col, slot = item // slots, item % slots

        @pl.when(occ_ref[slot, col] == 0)
        def _():
            out_ref[col, pl.ds(pl.multiple_of(slot * FREQ, FREQ), FREQ), :] = jnp.zeros((FREQ, 2 * FREQ), jnp.float32)

        @pl.when(occ_ref[slot, col] != 0)
        def _():
            m = spec_ref[col, pl.ds(pl.multiple_of(slot * FREQ, FREQ), FREQ), :]
            mr, mi = m[:, :FREQ], m[:, FREQ:]
            first = jnp.concatenate([jnp.concatenate([mr, mi] * 2, 1), jnp.concatenate([-mi, mr] * 2, 1)], 0)
            second = jnp.concatenate([jnp.concatenate([-mi, mr] * 2, 1), jnp.concatenate([-mr, -mi] * 2, 1)], 0)
            left_half = lax.broadcasted_iota(jnp.int32, (2 * FREQ, 128), 1) < 2 * FREQ
            for base in range(0, KERNELS, BATCH):
                parts = []
                for k in range(base, base + BATCH):
                    prod = kr_ref[k] * first + ki_ref[k] * second
                    high = prod.astype(jnp.bfloat16).astype(jnp.float32)
                    parts.append(jnp.where(left_half, prod, prod - high).astype(jnp.bfloat16))
                half = mixed_dot(jnp.concatenate(parts, 0), b_ref[0]).astype(jnp.bfloat16)
                p_ref[base * 2 * FREQ : (base + BATCH) * 2 * FREQ, :] = half
            intensity = jnp.zeros((BH, BW), jnp.float32)
            for base in range(0, KERNELS, BATCH):
                rhs = jnp.concatenate(
                    [p_ref[k * 2 * FREQ : (k + 1) * 2 * FREQ, :] for k in range(base, base + BATCH)], 1
                )
                field = mixed_dot(h_ref[0], rhs)
                e_ref[:, base * 2 * BW : base * 2 * BW + wide] = field
                square = field * field
                for lane in range(0, wide, BW):
                    intensity = intensity + square[:, lane : lane + BW]
            wanted = targ_ref[col, pl.ds(pl.multiple_of(slot * BH, BH), BH), :].astype(jnp.float32)
            resist = jax.nn.sigmoid(STEEP * (intensity - THRESHOLD))
            sens = (2.0 * 2.0 * STEEP) * (resist - wanted) * resist * (1.0 - resist)
            many = jnp.concatenate([sens] * (2 * BATCH), 1)
            sum_r = jnp.zeros((2 * FREQ, 128), jnp.float32)
            sum_i = jnp.zeros((2 * FREQ, 128), jnp.float32)
            for base in range(0, KERNELS, BATCH):
                cot = (e_ref[:, base * 2 * BW : base * 2 * BW + wide] * many).astype(jnp.bfloat16)
                pulled = mixed_dot(ht_ref[0], cot)
                high, low = two_parts(pulled)
                lhs = jnp.concatenate(
                    [
                        jnp.concatenate([high[:, at : at + 2 * BW], low[:, at : at + 2 * BW]], 1)
                        for at in range(0, wide, 2 * BW)
                    ],
                    0,
                )
                back = mixed_dot(lhs, g_ref[0])
                for n in range(BATCH):
                    z = back[n * 2 * FREQ : (n + 1) * 2 * FREQ]
                    sum_r = sum_r + kr_ref[base + n] * z
                    sum_i = sum_i + ki_ref[base + n] * z
            by_r = sum_r[:FREQ, : 2 * FREQ] + sum_r[FREQ:, 2 * FREQ :]
            by_i = sum_i[:FREQ, : 2 * FREQ] + sum_i[FREQ:, 2 * FREQ :]
            grad = jnp.concatenate(
                [by_r[:, :FREQ] + by_i[:, FREQ:], by_r[:, FREQ:] - by_i[:, :FREQ]], 1
            )
            out_ref[col, pl.ds(pl.multiple_of(slot * FREQ, FREQ), FREQ), :] = grad

        return carry

    lax.fori_loop(0, slots * GROUP, tile, 0)


def image(occ, spec, targ, kr, ki, place, slots):
    whole = lambda a: pl.BlockSpec(a.shape, lambda i, p, *_: (0,) * a.ndim)
    inv = jnp.asarray(INVERSE.reshape(2, BH, 2 * FREQ))
    inv_t = jnp.asarray(np.ascontiguousarray(INVERSE.reshape(2, BH, 2 * FREQ).transpose(0, 2, 1)))
    there, back = jnp.asarray(THERE), jnp.asarray(BACK)

    def body(place_ref, *refs):
        imaging(slots, *refs)

    return pl.pallas_call(
        body,
        grid_spec=pltpu.PrefetchScalarGridSpec(
            num_scalar_prefetch=1,
            grid=(1,),
            in_specs=[
                pl.BlockSpec(memory_space=pltpu.SMEM),
                whole(spec),
                whole(targ),
                whole(kr),
                whole(ki),
                pl.BlockSpec((1, BH, 2 * FREQ), lambda i, p: (p[0] % 2, 0, 0)),
                pl.BlockSpec((1, 2 * FREQ, BH), lambda i, p: (p[0] % 2, 0, 0)),
                pl.BlockSpec((1,) + THERE.shape[1:], lambda i, p: (p[0] // 2, 0, 0)),
                pl.BlockSpec((1,) + BACK.shape[1:], lambda i, p: (p[0] // 2, 0, 0)),
            ],
            out_specs=whole(spec),
            scratch_shapes=[
                pltpu.VMEM((KERNELS * 2 * FREQ, 2 * BW), jnp.bfloat16),
                pltpu.VMEM((BH, KERNELS * 2 * BW), jnp.float32),
            ],
        ),
        out_shape=jax.ShapeDtypeStruct(spec.shape, jnp.float32),
        compiler_params=pltpu.CompilerParams(vmem_limit_bytes=40 * 1024 * 1024),
    )(place, occ, spec, targ, kr, ki, inv, inv_t, there, back)


def shifted(value, axis, step):
    count = lax.axis_size(axis)
    return lax.ppermute(value, axis, [(i, i + step) for i in range(count) if 0 <= i + step < count])


def on_device(mask_field, target_field, occupancy, kernels, weights):
    height, width = mask_field.shape
    slots = height // TILE
    size = lax.axis_size("img")
    groups = [list(range(at, at + GROUP)) for at in range(0, size, GROUP)]
    band, column = lax.axis_index("own"), lax.axis_index("img")
    place = column % GROUP
    root = jnp.sqrt(weights)[:, None, None]
    dup = lambda part: jnp.tile(root * kernels[part], (1, 2, 4))
    kr, ki = dup(0), dup(1)
    occ = lax.dynamic_slice(occupancy, (band * slots, column - place), (slots, GROUP))
    targ = target_field.reshape(slots, 2, BH, TILE // BW, BW).transpose(3, 1, 0, 2, 4)
    targ = targ.reshape(GROUP, slots * BH, BW)
    targ = lax.all_to_all(targ, "img", 0, 0, axis_index_groups=groups)

    above = shifted(mask_field[height - AMBIT :], "own", 1)
    below = shifted(mask_field[:AMBIT], "own", -1)
    tall = jnp.concatenate([above, mask_field, below], 0)
    forward = jnp.asarray(FORWARD)
    upper = jnp.concatenate([mixed_dot(forward, tall[s * TILE : s * TILE + PAD]) for s in range(slots)], 0)
    upper = upper.astype(jnp.bfloat16)
    across = jnp.asarray(spread(1))
    three = mixed_dot(upper, across.T)
    spec = three[:, 64:128] + shifted(three[:, :64], "img", -1) + shifted(three[:, 128:], "img", 1)
    spec = spec.reshape(slots, 2, FREQ, 2, FREQ)
    spec = jnp.concatenate([spec[:, 0, :, 0] - spec[:, 1, :, 1], spec[:, 0, :, 1] + spec[:, 1, :, 0]], -1)
    spec = lax.all_gather(spec.reshape(slots * FREQ, 2 * FREQ), "img", axis_index_groups=groups)

    grad = image(occ, spec, targ, kr, ki, place.reshape(1).astype(jnp.int32), slots)
    grad = lax.all_to_all(grad, "img", 0, 0, axis_index_groups=groups).sum(0)
    three = jnp.concatenate([shifted(grad, "img", 1), grad, shifted(grad, "img", -1)], 1)
    three = three.reshape(slots, FREQ, 3, 2, FREQ)
    gr, gi = three[:, :, :, 0], three[:, :, :, 1]
    both = jnp.stack([jnp.stack([gr, gi], 3), jnp.stack([gi, -gr], 3)], 1)
    high, low = two_parts(both.reshape(slots * 2 * FREQ, 6 * FREQ))
    lowered = (mixed_dot(high, across) + mixed_dot(low, across)).astype(jnp.bfloat16)
    from_above = shifted(lowered[-2 * FREQ :], "own", 1)
    from_below = shifted(lowered[: 2 * FREQ], "own", -1)
    lowered = jnp.concatenate([from_above, lowered, from_below], 0)
    values = mask_field.astype(jnp.float32)
    penalty = GAMMA * 4.0 * values * (values * values - 1.0)
    return mixed_dot(jnp.asarray(np.ascontiguousarray(spread(slots).T)), lowered) + penalty


def solution(mesh):
    return jax.shard_map(
        on_device,
        mesh=mesh,
        in_specs=(P("own", "img"), P("own", "img"), P(), P(), P()),
        out_specs=P("own", "img"),
        check_vma=False,
    )
```

profile of v0, /device:TPU:11, one launch (start us, length us, event | category | flops | bytes accessed | tf_op | source)
XLA Modules:
  0.0 108.5 jit_solution(9372366690902804802)
XLA Ops:
  0.0 0.9 fusion.18
  0.9 3.2 %collective-permute-start = (bf16[64,512]{1,0:T(8,128)(2,1)S(1)}, bf16[64,512]{1,0:T(8,128)(2,1)S(1)}, u32[]{:S(2)}, u32[]{:S(2)}) collective-permute-start(bf16[64,512]{1,0:T(8,128)(2,1)S(1)} %get-tuple-element.5), channel_id=1, source_target_pairs={{0,8},{8,16},{16,24},{1,9},{9,17},{17,25},{2,10},{10,18},{18,26},{... | collective-permute-start | bytes 196616 | tf_op jit(solution)/shard_map/ppermute | solution.py:185
  4.1 2.1 %collective-permute-start.1 = (bf16[64,512]{1,0:T(8,128)(2,1)S(1)}, bf16[64,512]{1,0:T(8,128)(2,1)S(1)}, u32[]{:S(2)}, u32[]{:S(2)}) collective-permute-start(bf16[64,512]{1,0:T(8,128)(2,1)S(1)} %get-tuple-element.6), channel_id=1, source_target_pairs={{8,0},{16,8},{24,16},{9,1},{17,9},{25,17},{10,2},{18,10},{26,18},{... | collective-permute-start | bytes 196616 | tf_op jit(solution)/shard_map/ppermute | solution.py:185
  6.2 1.3 %reshape.76 = bf16[2,2,256,4,128]{4,3,2,1,0:T(4,128)(2,1)S(1)} reshape(bf16[1024,512]{1,0:T(8,128)(2,1)} %param.13) | data formatting | bytes 2097152 | tf_op jit(solution)/shard_map/reshape | solution.py:199
  7.6 1.2 %copy.37 = bf16[2,2,256,4,128]{4,2,0,1,3:T(8,128)(2,1)} copy(bf16[2,2,256,4,128]{4,3,2,1,0:T(4,128)(2,1)S(1)} %reshape.76) | data formatting | bytes 2097152 | tf_op jit(solution)/shard_map/reshape | solution.py:199
  8.7 5.3 %all-to-all-start = ((bf16[8,512,128]{2,1,0:T(8,128)(2,1)}), bf16[8,512,128]{2,1,0:T(8,128)(2,1)S(1)}, u32[]{:S(2)}, u32[]{:S(2)}) async-start(bf16[8,512,128]{2,1,0:T(8,128)(2,1)} %bitcast.6), calls=%async_computation | async-start | bytes 2097152 | tf_op jit(solution)/shard_map/all_to_all | solution.py:201
  14.0 1.3 %bitcast_multiply_fusion = (f32[24,32,32]{2,1,0:T(8,128)S(1)}, f32[24,32,32]{2,1,0:T(8,128)S(1)}) fusion(f32[2,24,32,32]{3,2,1,0:T(8,128)} %param.15, f32[24]{0:T(128)S(1)} %sqrt.3), kind=kLoop, calls=%fused_computation.15 | loop fusion | flops 49152 | bytes 393312 | tf_op jit(solution)/shard_map/mul | solution.py:196
  15.3 0.2 fusion.3
  15.6 0.2 fusion.4
  15.8 0.2 fusion.7
  16.1 2.3 %collective-permute-start.2 = (f32[128,64]{0,1:T(8,128)S(1)}, f32[128,64]{0,1:T(8,128)S(1)}, u32[]{:S(2)}, u32[]{:S(2)}) collective-permute-start(f32[128,64]{0,1:T(8,128)S(1)} %get-tuple-element.15), channel_id=1, source_target_pairs={{1,0},{2,1},{3,2},{4,3},{5,4},{6,5},{7,6},{9,8},{10,9},{11,10},{12... | collective-permute-start | bytes 98312 | tf_op jit(solution)/shard_map/ppermute | solution.py:185
  18.3 4.2 %collective-permute-start.3 = (f32[128,64]{0,1:T(8,128)S(1)}, f32[128,64]{0,1:T(8,128)S(1)}, u32[]{:S(2)}, u32[]{:S(2)}) collective-permute-start(f32[128,64]{0,1:T(8,128)S(1)} %get-tuple-element.16), channel_id=1, source_target_pairs={{0,1},{1,2},{2,3},{3,4},{4,5},{5,6},{6,7},{8,9},{9,10},{10,11},{11... | collective-permute-start | bytes 98312 | tf_op jit(solution)/shard_map/ppermute | solution.py:185
  22.6 2.4 %tile.20 = f32[24,2,32,4,32]{4,3,2,1,0:T(4,128)} broadcast(f32[24,32,32]{2,1,0:T(8,128)S(1)} %get-tuple-element.7), dimensions={0,2,4} | broadcast | bytes 884736 | tf_op jit(solution)/shard_map/tile | solution.py:196
  25.0 2.8 %tile.21.refs_4_ = f32[24,64,128]{2,1,0:T(8,128)S(1)} reshape(f32[24,2,32,4,32]{4,3,2,1,0:T(4,128)} %tile.20) | data formatting | bytes 1572864 | tf_op jit(solution)/shard_map/tile | solution.py:196
  27.8 2.4 %tile.8 = f32[24,2,32,4,32]{4,3,2,1,0:T(4,128)} broadcast(f32[24,32,32]{2,1,0:T(8,128)S(1)} %get-tuple-element.8), dimensions={0,2,4} | broadcast | bytes 884736 | tf_op jit(solution)/shard_map/tile | solution.py:196
  30.2 2.9 %tile.9.refs_3_ = f32[24,64,128]{2,1,0:T(8,128)S(1)} reshape(f32[24,2,32,4,32]{4,3,2,1,0:T(4,128)} %tile.8) | data formatting | bytes 1572864 | tf_op jit(solution)/shard_map/tile | solution.py:196
  33.1 0.2 reshape.75
  33.5 0.1 pad_maximum_fusion.6
  33.6 8.1 %all_gather.3.refs_1_ = f32[8,64,64]{2,1,0:T(8,128)S(1)} all-gather(f32[1,64,64]{2,1,0:T(8,128)S(1)} %pad_maximum_fusion.6), channel_id=1, replica_groups={{0,1,2,3,4,5,6,7},{8,9,10,11,12,13,14,15},{16,17,18,19,20,21,22,23},{24..., dimensions={0}, use_global_device_ids=true | all-gather | bytes 147456 | tf_op jit(solution)/shard_map/all_gather | solution.py:214
  41.8 1.0 copy-done.1
  42.8 0.8 copy-done.4
  43.6 23.5 %shard_map.118 = f32[8,64,64]{2,1,0:T(8,128)S(1)} custom-call(s32[1]{0:T(128)} %bitcast.place_ref, s32[2,8]{1,0:T(2,128)S(1)} %constant_dynamic-slice_fusion.refs_0_, f32[8,64,64]{2,1,0:T(8,128)S(1)} %all_gather.3.refs_1_, bf16[8,512,128]{2,1,0:T(8,128)(2,1)S(1)} %all-to-all-done.refs_2_, f32[24,64,128]{2,1,0:T(8,128)S(1)} %tile.9.refs_3_, ...), custom_call_target="tpu_custom_call" | custom-call | tf_op jit(solution)/shard_map/pallas_call | solution.py:156
  67.1 0.2 reshape.80
  67.3 6.7 %all_to_all.10 = f32[8,1,4096]{2,1,0:T(1,128)S(1)} all-to-all(f32[8,1,4096]{2,1,0:T(1,128)S(1)} %reshape.80), channel_id=1, replica_groups={{0,1,2,3,4,5,6,7},{8,9,10,11,12,13,14,15},{16,17,18,19,20,21,22,23},{24..., dimensions={0} | all-to-all | bytes 262144 | tf_op jit(solution)/shard_map/all_to_all | solution.py:217
  74.1 0.5 broadcast.19
  74.6 1.0 reduce
  75.5 0.1 reshape.81
  75.7 3.7 %collective-permute-start.4 = (f32[64,64]{1,0:T(8,128)S(1)}, f32[64,64]{1,0:T(8,128)S(1)}, u32[]{:S(2)}, u32[]{:S(2)}) collective-permute-start(f32[64,64]{1,0:T(8,128)S(1)} %reduce_sum.9), channel_id=1, source_target_pairs={{0,1},{1,2},{2,3},{3,4},{4,5},{5,6},{6,7},{8,9},{9,10},{10,11},{11... | collective-permute-start | bytes 49160 | tf_op jit(solution)/shard_map/ppermute | solution.py:185
  79.4 1.9 %collective-permute-start.5 = (f32[64,64]{1,0:T(8,128)S(1)}, f32[64,64]{1,0:T(8,128)S(1)}, u32[]{:S(2)}, u32[]{:S(2)}) collective-permute-start(f32[64,64]{1,0:T(8,128)S(1)} %reduce_sum.9), channel_id=1, source_target_pairs={{1,0},{2,1},{3,2},{4,3},{5,4},{6,5},{7,6},{9,8},{10,9},{11,10},{12... | collective-permute-start | bytes 49160 | tf_op jit(solution)/shard_map/ppermute | solution.py:185
  81.3 0.5 copy.39
  81.9 3.6 %collective-permute-done.5 = f32[64,64]{1,0:T(8,128)S(1)} collective-permute-done((f32[64,64]{1,0:T(8,128)S(1)}, f32[64,64]{1,0:T(8,128)S(1)}, u32[]{:S(2)}, u32[]{:S(2)}) %collective-permute-start.5) | collective-permute-done | bytes 16416 | tf_op jit(solution)/shard_map/ppermute | solution.py:185
  85.5 0.1 pad_maximum_fusion.5
  85.6 0.2 reshape.78
  85.8 0.2 stack.14
  86.0 0.2 fusion.19
  86.1 0.2 maximum_bitcast_fusion
  86.4 0.2 pad_maximum_fusion.4
  86.6 0.3 copy.38
  86.9 0.3 reshape.79
  87.3 0.2 fusion.13
  87.5 0.2 fusion.2
  87.7 3.3 %collective-permute-start.6 = (bf16[64,512]{1,0:T(8,128)(2,1)S(1)}, bf16[64,512]{1,0:T(8,128)(2,1)S(1)}, u32[]{:S(2)}, u32[]{:S(2)}) collective-permute-start(bf16[64,512]{1,0:T(8,128)(2,1)S(1)} %get-tuple-element.11), channel_id=1, source_target_pairs={{0,8},{8,16},{16,24},{1,9},{9,17},{17,25},{2,10},{10,18},{18,26},{... | collective-permute-start | bytes 196616 | tf_op jit(solution)/shard_map/ppermute | solution.py:185
  91.1 0.5 fusion.23
  91.5 2.1 %collective-permute-start.7 = (bf16[64,512]{1,0:T(8,128)(2,1)S(1)}, bf16[64,512]{1,0:T(8,128)(2,1)S(1)}, u32[]{:S(2)}, u32[]{:S(2)}) collective-permute-start(bf16[64,512]{1,0:T(8,128)(2,1)S(1)} %get-tuple-element.12), channel_id=1, source_target_pairs={{8,0},{16,8},{24,16},{9,1},{17,9},{25,17},{10,2},{18,10},{26,18},{... | collective-permute-start | bytes 196616 | tf_op jit(solution)/shard_map/ppermute | solution.py:185
  93.7 0.5 fusion.22
  94.1 11.9 %collective-permute-done.7 = bf16[64,512]{1,0:T(8,128)(2,1)S(1)} collective-permute-done((bf16[64,512]{1,0:T(8,128)(2,1)S(1)}, bf16[64,512]{1,0:T(8,128)(2,1)S(1)}, u32[]{:S(2)}, u32[]{:S(2)}) %collective-permute-start.7) | collective-permute-done | bytes 65568 | tf_op jit(solution)/shard_map/ppermute | solution.py:185
  106.0 0.7 fusion.1
  106.7 1.8 %copy.40 = f32[1024,512]{1,0:T(8,128)} copy(f32[1024,512]{0,1:T(8,128)S(1)} %fusion.1) | data formatting | bytes 4194304 | tf_op jit(solution)/shard_map/add | solution.py:229
  (42 shorter events, 0.4 us)
Async XLA Ops:
  0.0 22.5 %copy-start = (s32[8,8]{1,0:T(8,128)S(1)}, s32[8,8]{1,0:T(8,128)}, u32[]{:S(2)}) copy-start(s32[8,8]{1,0:T(8,128)} %param.14) | copy-start | bytes 772
  0.9 14.4 %collective-permute-start = (bf16[64,512]{1,0:T(8,128)(2,1)S(1)}, bf16[64,512]{1,0:T(8,128)(2,1)S(1)}, u32[]{:S(2)}, u32[]{:S(2)}) collective-permute-start(bf16[64,512]{1,0:T(8,128)(2,1)S(1)} %get-tuple-element.5), channel_id=1, source_target_pairs={{0,8},{8,16},{16,24},{1,9},{9,17},{17,25},{2,10},{10,18},{18,26},{... | collective-permute-start | bytes 196616 | tf_op jit(solution)/shard_map/ppermute | solution.py:185
  4.1 11.5 %collective-permute-start.1 = (bf16[64,512]{1,0:T(8,128)(2,1)S(1)}, bf16[64,512]{1,0:T(8,128)(2,1)S(1)}, u32[]{:S(2)}, u32[]{:S(2)}) collective-permute-start(bf16[64,512]{1,0:T(8,128)(2,1)S(1)} %get-tuple-element.6), channel_id=1, source_target_pairs={{8,0},{16,8},{24,16},{9,1},{17,9},{25,17},{10,2},{18,10},{26,18},{... | collective-permute-start | bytes 196616 | tf_op jit(solution)/shard_map/ppermute | solution.py:185
  7.6 6.5 %copy-start.13 = (f32[24]{0:T(128)S(1)}, f32[24]{0:T(128)}, u32[]{:S(2)}) copy-start(f32[24]{0:T(128)} %param.16) | copy-start | bytes 292
  8.7 6.6 %copy-start.5 = (bf16[1024,512]{1,0:T(8,128)(2,1)S(1)}, bf16[1024,512]{1,0:T(8,128)(2,1)}, u32[]{:S(2)}) copy-start(bf16[1024,512]{1,0:T(8,128)(2,1)} %param.12) | copy-start | bytes 3145732
  8.7 6.6 %copy-start.9 = (bf16[64,640]{1,0:T(8,128)(2,1)S(1)}, bf16[64,640]{1,0:T(8,128)(2,1)}, u32[]{:S(2)}) copy-start(bf16[64,640]{1,0:T(8,128)(2,1)} %constant.44.clone) | copy-start | bytes 245764
  8.7 33.0 %all-to-all-start = ((bf16[8,512,128]{2,1,0:T(8,128)(2,1)}), bf16[8,512,128]{2,1,0:T(8,128)(2,1)S(1)}, u32[]{:S(2)}, u32[]{:S(2)}) async-start(bf16[8,512,128]{2,1,0:T(8,128)(2,1)} %bitcast.6), calls=%async_computation | async-start | bytes 2097152 | tf_op jit(solution)/shard_map/all_to_all | solution.py:201
  14.0 1.8 %copy-start.7 = (bf16[192,512]{1,0:T(8,128)(2,1)S(1)}, bf16[192,512]{1,0:T(8,128)(2,1)}, u32[]{:S(2)}) copy-start(bf16[192,512]{1,0:T(8,128)(2,1)} %constant.45.clone) | copy-start | bytes 589828
  16.1 17.0 %collective-permute-start.2 = (f32[128,64]{0,1:T(8,128)S(1)}, f32[128,64]{0,1:T(8,128)S(1)}, u32[]{:S(2)}, u32[]{:S(2)}) collective-permute-start(f32[128,64]{0,1:T(8,128)S(1)} %get-tuple-element.15), channel_id=1, source_target_pairs={{1,0},{2,1},{3,2},{4,3},{5,4},{6,5},{7,6},{9,8},{10,9},{11,10},{12... | collective-permute-start | bytes 98312 | tf_op jit(solution)/shard_map/ppermute | solution.py:185
  18.3 14.8 %collective-permute-start.3 = (f32[128,64]{0,1:T(8,128)S(1)}, f32[128,64]{0,1:T(8,128)S(1)}, u32[]{:S(2)}, u32[]{:S(2)}) collective-permute-start(f32[128,64]{0,1:T(8,128)S(1)} %get-tuple-element.16), channel_id=1, source_target_pairs={{0,1},{1,2},{2,3},{3,4},{4,5},{5,6},{6,7},{8,9},{9,10},{10,11},{11... | collective-permute-start | bytes 98312 | tf_op jit(solution)/shard_map/ppermute | solution.py:185
  30.2 11.5 %copy-start.2 = (bf16[4,128,256]{2,1,0:T(8,128)(2,1)S(1)}, bf16[4,128,256]{2,1,0:T(8,128)(2,1)}, u32[]{:S(2)}) copy-start(bf16[4,128,256]{2,1,0:T(8,128)(2,1)} %constant.48.clone.refs_7_) | copy-start | bytes 786436
  30.2 11.5 %copy-start.3 = (bf16[2,256,64]{2,1,0:T(8,128)(2,1)S(1)}, bf16[2,256,64]{2,1,0:T(8,128)(2,1)}, u32[]{:S(2)}) copy-start(bf16[2,256,64]{2,1,0:T(8,128)(2,1)} %constant.46.clone.refs_5_) | copy-start | bytes 196612
  41.7 1.0 copy-start.1
  42.8 0.8 copy-start.4
  67.1 14.2 %copy-start.6 = (bf16[1024,512]{1,0:T(8,128)(2,1)S(1)}, bf16[1024,512]{1,0:T(8,128)(2,1)}, u32[]{:S(2)}) copy-start(bf16[1024,512]{1,0:T(8,128)(2,1)} %param.12) | copy-start | bytes 3145732
  75.7 6.2 %collective-permute-start.4 = (f32[64,64]{1,0:T(8,128)S(1)}, f32[64,64]{1,0:T(8,128)S(1)}, u32[]{:S(2)}, u32[]{:S(2)}) collective-permute-start(f32[64,64]{1,0:T(8,128)S(1)} %reduce_sum.9), channel_id=1, source_target_pairs={{0,1},{1,2},{2,3},{3,4},{4,5},{5,6},{6,7},{8,9},{9,10},{10,11},{11... | collective-permute-start | bytes 49160 | tf_op jit(solution)/shard_map/ppermute | solution.py:185
  79.4 6.1 %collective-permute-start.5 = (f32[64,64]{1,0:T(8,128)S(1)}, f32[64,64]{1,0:T(8,128)S(1)}, u32[]{:S(2)}, u32[]{:S(2)}) collective-permute-start(f32[64,64]{1,0:T(8,128)S(1)} %reduce_sum.9), channel_id=1, source_target_pairs={{1,0},{2,1},{3,2},{4,3},{5,4},{6,5},{7,6},{9,8},{10,9},{11,10},{12... | collective-permute-start | bytes 49160 | tf_op jit(solution)/shard_map/ppermute | solution.py:185
  81.9 5.4 %copy-start.8 = (bf16[192,512]{1,0:T(8,128)(2,1)S(1)}, bf16[192,512]{1,0:T(8,128)(2,1)}, u32[]{:S(2)}) copy-start(bf16[192,512]{1,0:T(8,128)(2,1)} %constant.45.clone) | copy-start | bytes 589828
  86.0 5.1 %copy-start.11 = (bf16[1024,128]{1,0:T(8,128)(2,1)S(1)}, bf16[1024,128]{1,0:T(8,128)(2,1)}, u32[]{:S(2)}) copy-start(bf16[1024,128]{1,0:T(8,128)(2,1)} %constant.52) | copy-start | bytes 786436
  87.3 6.4 %copy-start.10 = (bf16[1024,64]{1,0:T(8,128)(2,1)S(1)}, bf16[1024,64]{1,0:T(8,128)(2,1)}, u32[]{:S(2)}) copy-start(bf16[1024,64]{1,0:T(8,128)(2,1)} %constant.51) | copy-start | bytes 393220
  87.7 18.3 %copy-start.12 = (bf16[1024,64]{1,0:T(8,128)(2,1)S(1)}, bf16[1024,64]{1,0:T(8,128)(2,1)}, u32[]{:S(2)}) copy-start(bf16[1024,64]{1,0:T(8,128)(2,1)} %constant.53) | copy-start | bytes 393220
  87.7 5.9 %collective-permute-start.6 = (bf16[64,512]{1,0:T(8,128)(2,1)S(1)}, bf16[64,512]{1,0:T(8,128)(2,1)S(1)}, u32[]{:S(2)}, u32[]{:S(2)}) collective-permute-start(bf16[64,512]{1,0:T(8,128)(2,1)S(1)} %get-tuple-element.11), channel_id=1, source_target_pairs={{0,8},{8,16},{16,24},{1,9},{9,17},{17,25},{2,10},{10,18},{18,26},{... | collective-permute-start | bytes 196616 | tf_op jit(solution)/shard_map/ppermute | solution.py:185
  91.5 14.5 %collective-permute-start.7 = (bf16[64,512]{1,0:T(8,128)(2,1)S(1)}, bf16[64,512]{1,0:T(8,128)(2,1)S(1)}, u32[]{:S(2)}, u32[]{:S(2)}) collective-permute-start(bf16[64,512]{1,0:T(8,128)(2,1)S(1)} %get-tuple-element.12), channel_id=1, source_target_pairs={{8,0},{16,8},{24,16},{9,1},{17,9},{25,17},{10,2},{18,10},{26,18},{... | collective-permute-start | bytes 196616 | tf_op jit(solution)/shard_map/ppermute | solution.py:185
where the time goes:
time: 108 us; the launch traced here: 109 us
  starting transfers between devices  28.1 us (26%)
  Pallas kernels  23.5 us (22%)
  local copies, waits for them, and re-layouts  20.3 us (19%)
  waiting for transfers between devices  15.6 us (14%)
  blocking collectives  14.8 us (14%)
  other arithmetic  3.08 us (3%)
  matrix products  2.68 us (2%)
    pallas_call x1, Pallas kernels, image(): pl.pallas_call(body, grid_spec=pltpu.PrefetchScalarGridSpec(num_scalar_pr...  23.5 us
    ppermute x8, starting transfers between devices, shifted(): lax.ppermute(value, axis, [(i, i + step) for i in range(count) if 0 <= i...  22.8 us
    ppermute x8, waiting for transfers between devices, shifted(): lax.ppermute(value, axis, [(i, i + step) for i in range(count) if 0 <= i...  15.6 us
    another operation x4, local copies, waits for them, and re-layouts, on_device(): dup = lambda part: jnp.tile(root * kernels[part], (1, 2, 4))  10.5 us
    all_gather x1, blocking collectives, on_device(): lax.all_gather(spec.reshape(slots * FREQ, 2 * FREQ), 'img', axis_index_gr...  8.12 us
    all_to_all x1, blocking collectives, on_device(): grad = lax.all_to_all(grad, 'img', 0, 0, axis_index_groups=groups).sum(0)  6.72 us
    all_to_all x1, starting transfers between devices, on_device(): targ = lax.all_to_all(targ, 'img', 0, 0, axis_index_groups=groups)  5.26 us
    unnamed x31, local copies, waits for them, and re-layouts  2.75 us
  transfers between devices with their start and end apart: 9, of which 2 were waited for; matrix products, arithmetic and copies ran while one was open for 16% of the time, Pallas kernels for 0%

commit v1 on v0

v1 whole, which is shorter than its diff:
```python
import math

import jax
import jax.numpy as jnp
import numpy as np
from jax import lax
from jax.experimental import pallas as pl
from jax.experimental.pallas import tpu as pltpu
from jax.sharding import PartitionSpec as P

TILE = 512
AMBIT = 64
FREQ = 32
KERNELS = 24
PAD = 640
STEEP = 2.0
THRESHOLD = 1.5
GAMMA = 0.25
GRID = 64


def tables():
    freqs = np.arange(FREQ) - FREQ // 2
    turn = np.float32(2.0 * math.pi / PAD)
    phase = ((freqs[:, None] * np.arange(PAD)[None, :]) % PAD).astype(np.float32) * turn
    bf = lambda a: np.asarray(a, np.float32).astype(jnp.bfloat16)
    return (
        bf(np.cos(phase) / np.float32(math.sqrt(PAD))),
        bf(-np.sin(phase) / np.float32(math.sqrt(PAD))),
    )


FC, FS = tables()
FORWARD = np.concatenate([FC, FS], 0)


def spread(count):
    length = count * TILE
    out = np.zeros((count + 2, 2 * FREQ, length), jnp.bfloat16)
    for tile in range(-1, count + 1):
        start = tile * TILE - AMBIT
        low, high = max(start, 0), min(start + PAD, length)
        out[tile + 1, :, low:high] = FORWARD[:, low - start : high - start]
    return out.reshape(-1, length)


def two_tables(table):
    high = np.asarray(table).astype(jnp.bfloat16)
    return high, (table - high.astype(np.float64)).astype(jnp.bfloat16)


def grid_tables():
    freqs = np.arange(FREQ) - FREQ // 2
    turn = 2.0 * math.pi * (np.arange(GRID)[:, None] * freqs[None, :]) / GRID
    c, s = np.cos(turn) / math.sqrt(FREQ), np.sin(turn) / math.sqrt(FREQ)
    zero = np.zeros((2 * FREQ, 2 * GRID))
    one = np.block([[c.T, s.T], [-s.T, c.T]])
    there_high, there_low = two_tables(np.block([[one, zero], [zero, one]]))
    there = np.concatenate([there_high, there_high, there_low], 0)
    high, low = two_tables(np.concatenate([c, s], 1))
    rows = np.concatenate([high, high, low], 1)
    rows_back = np.concatenate([high.T, high.T, low.T], 1)
    zero = np.zeros((2 * GRID, 2 * FREQ))
    parts = []
    for adj in (np.block([[c, -s], [s, c]]), np.block([[-s, -c], [c, -s]])):
        parts.append(np.block([[adj, zero], [zero, adj]]))
    high, low = two_tables(np.concatenate(parts, 0))
    back = np.concatenate([high, high, low], 0)
    waves = np.arange(-(FREQ - 1), FREQ)
    apart = (np.arange(TILE) + AMBIT)[:, None] / PAD - np.arange(GRID)[None, :] / GRID
    fine = np.cos(2.0 * math.pi * apart[:, :, None] * waves).sum(-1) / GRID
    high, low = two_tables(fine)
    up = np.concatenate([high, high, low, np.zeros_like(low)], 1)
    down = np.concatenate([high.T, low.T], 0)
    down_cols = np.concatenate([high, high, low, low], 1)
    return there, rows, rows_back, back, up, np.ascontiguousarray(up.T), down, down_cols


def exchange_tables(slots):
    rows = spread(slots).reshape(slots + 2, 2, FREQ, -1)[1:-1].transpose(1, 0, 2, 3).reshape(2 * slots * FREQ, -1)
    edge = np.zeros((2, slots, FREQ, 2 * AMBIT), jnp.bfloat16)
    both = FORWARD.reshape(2, FREQ, PAD)
    edge[:, 0, :, :AMBIT] = both[:, :, :AMBIT]
    edge[:, -1, :, AMBIT:] = both[:, :, -AMBIT:]
    near = spread(1).reshape(3, 2, FREQ, TILE)
    cols = []
    for which in (1, 1, 0, 2):
        c, s = near[which].astype(np.float32)
        cols.append(np.block([[c.T, s.T], [-s.T, c.T]]))
    return rows, edge.reshape(2 * slots * FREQ, -1), np.concatenate(cols, 1).astype(jnp.bfloat16)


def lowering_tables():
    near = spread(1).reshape(3, 2, FREQ, TILE).astype(np.float32)
    full = [np.block([[c, -s], [s, c]]) for c, s in near]
    cut = [np.block([[c, -s], [s, c]]) for c, s in (near[0][:, :, :128], near[2][:, :, -128:])]
    twice = lambda a: np.concatenate([a, a], 0).astype(jnp.bfloat16)
    return twice(full[1]), np.stack([twice(cut[0]), twice(cut[1])])


def mixed_dot(left, right):
    return jnp.dot(left, right, preferred_element_type=jnp.float32)


def two_parts(value):
    high = value.astype(jnp.bfloat16)
    return high, (value - high.astype(jnp.float32)).astype(jnp.bfloat16)


MESH = pl.DeviceIdType.MESH
VMEM = pl.BlockSpec(memory_space=pltpu.VMEM)
NEAR = [(dy, dx) for dy in (-1, 0, 1) for dx in (-1, 0, 1) if (dy, dx) != (0, 0)]


class Place:
    def __init__(self, bands, size):
        self.bands, self.size = bands, size
        self.band, self.column = lax.axis_index("own"), lax.axis_index("img")

    def near(self, dy, dx):
        row, col = self.band + dy, self.column + dx
        there = (row >= 0) & (row < self.bands) & (col >= 0) & (col < self.size)
        return there, (row, col)

    def greet(self, offsets):
        barrier = pltpu.get_barrier_semaphore()
        count = jnp.int32(0)
        for offset in offsets:
            there, device = self.near(*offset)
            count = count + there.astype(jnp.int32)

            @pl.when(there)
            def _():
                pl.semaphore_signal(barrier, inc=1, device_id=device, device_id_type=MESH)

        pl.semaphore_wait(barrier, count)


def push(src, dst, send, recv, device):
    return pltpu.make_async_remote_copy(
        src_ref=src, dst_ref=dst, send_sem=send, recv_sem=recv, device_id=device, device_id_type=MESH
    )


def swapped(value, lane):
    return jnp.where(lane % 64 < 32, pltpu.roll(value, 96, 1), pltpu.roll(value, 32, 1))


def spectrum_gradients(m, flags, wanted, kern_ref, root_ref, t, sens_ref):
    lane = lax.broadcasted_iota(jnp.int32, (FREQ, 128), 1)
    sign = jnp.where(lane % 64 < 32, -1.0, 1.0)
    n = sign * swapped(m, lane)
    spectra, parts = [], []
    for k in range(KERNELS):
        kr, ki = [jnp.concatenate([kern_ref[part, k]] * 4, 1) * root_ref[k] for part in (0, 1)]
        spectra.append((kr, ki))
        parts += [kr * m + ki * n, kr * n - ki * m]
    high, low = two_parts(jnp.concatenate(parts, 0))
    half = mixed_dot(jnp.concatenate([high, low, high], 1), t["there"][...])
    high, low = two_parts(half)
    fields = []
    total = jnp.zeros((GRID, 256), jnp.float32)
    for k in range(KERNELS):
        at = slice(k * 64, (k + 1) * 64)
        field = mixed_dot(t["rows"][...], jnp.concatenate([high[at], low[at], high[at]], 0))
        fields.append(field)
        total = total + field * field
    coarse = jnp.concatenate([total[:, :128], total[:, 128:]], 0)
    coarse = coarse + pltpu.roll(coarse, 64, 1)
    high, low = two_parts(coarse)
    first = lax.broadcasted_iota(jnp.int32, (2 * GRID, 128), 1) < 64
    zero = jnp.zeros((2 * GRID, 128), jnp.float32)
    high32, low32 = high.astype(jnp.float32), low.astype(jnp.float32)
    lhs = jnp.concatenate([jnp.where(first, high32, low32), jnp.where(first, high32, zero)], 1).astype(jnp.bfloat16)
    across = mixed_dot(lhs, t["up_t"][...])
    high, low = two_parts(across)
    rows = 128
    for slot in range(2):
        at = slice(slot * GRID, (slot + 1) * GRID)
        rhs = jnp.concatenate([high[at], low[at], high[at], jnp.zeros((GRID, TILE), jnp.bfloat16)], 0)
        for start in range(0, TILE, rows):
            intensity = mixed_dot(t["up"][start : start + rows, :], rhs)
            bend = jnp.tanh((0.5 * STEEP) * (intensity - THRESHOLD))
            goal = wanted[slot * TILE + start : slot * TILE + start + rows, :].astype(jnp.float32)
            sens = (0.5 * STEEP) * (1.0 + bend - 2.0 * goal) * (1.0 - bend * bend)
            sens_ref[start : start + rows, slot * TILE : (slot + 1) * TILE] = sens.astype(jnp.bfloat16)
    folded = mixed_dot(t["down"][...], sens_ref[...])
    folded = folded[:GRID] + folded[GRID:]
    high, low = two_parts(jnp.concatenate([folded[:, :TILE], folded[:, TILE:]], 0))
    grid = mixed_dot(jnp.concatenate([high, low], 0), t["down_cols"][...])
    grid = grid[:128, :128] + grid[:128, 128:] + grid[128:, :128]
    weight = jnp.concatenate([grid[:GRID], grid[GRID:]], 1)
    tops, bottoms = [], []
    for k in range(KERNELS):
        high, low = two_parts(fields[k] * weight)
        pulled = mixed_dot(t["rows_back"][...], jnp.concatenate([high, low, high], 0))
        tops.append(pulled[:FREQ])
        bottoms.append(pulled[FREQ:])
    high, low = two_parts(jnp.concatenate([jnp.concatenate(tops, 0), jnp.concatenate(bottoms, 0)], 1))
    back = mixed_dot(jnp.concatenate([high, low, high], 1), t["back"][...])
    sum_r = jnp.zeros((FREQ, 128), jnp.float32)
    sum_i = jnp.zeros((FREQ, 128), jnp.float32)
    for k in range(KERNELS):
        z = back[k * FREQ : (k + 1) * FREQ]
        sum_r = sum_r + spectra[k][0] * z
        sum_i = sum_i + spectra[k][1] * z
    grad = sum_r - sign * swapped(sum_i, lane)
    return jnp.where(jnp.where(lane < 64, flags[0], flags[1]) > 0, grad, 0.0)


NAMES = ["there", "rows", "rows_back", "back", "up", "up_t", "down", "down_cols"]
COPIED = ["mask", "row_table", "edge", "cols", "there", "rows", "up_t", "up", "target", "down", "down_cols", "rows_back", "back", "own", "beside"]


def whole(bands, size, slots, shapes, root_ref, occ_ref, kern_ref, *refs):
    count = len(COPIED)
    sources = dict(zip(COPIED, refs[:count]))
    low_ref = refs[count]
    held = dict(zip(COPIED, refs[count + 1 : 2 * count + 1]))
    (sens_ref, halo, out_msg, side, full, near, copy_sem,
     halo_send, halo_recv, side_send, side_recv, near_send, near_recv) = refs[2 * count + 1 :]
    at = Place(bands, size)
    height = slots * TILE
    copies = {}
    for n, name in enumerate(COPIED):
        copies[name] = pltpu.make_async_copy(sources[name], held[name], copy_sem.at[n])
        copies[name].start()
    at.greet(NEAR)

    vertical = []
    for n, dy in enumerate((-1, 1)):
        there, device = at.near(dy, 0)
        src = sources["mask"].at[pl.ds(0 if dy < 0 else height - AMBIT, AMBIT)]
        copy = push(src, halo.at[pl.ds((1 - n) * AMBIT, AMBIT)], halo_send.at[n], halo_recv.at[n], device)
        vertical.append((there, copy))
        pl.when(there)(copy.start)
    for name in ("mask", "row_table", "edge", "cols"):
        copies[name].wait()
    upper = mixed_dot(held["row_table"][...], held["mask"][...])
    for n, (there, copy) in enumerate(vertical):
        source, _ = at.near(1 if n == 0 else -1, 0)
        pl.when(source)(copy.wait_recv)

        @pl.when(jnp.logical_not(source))
        def _():
            halo[(1 - n) * AMBIT : (2 - n) * AMBIT, :] = jnp.zeros((AMBIT, TILE), jnp.bfloat16)

    upper = (upper + mixed_dot(held["edge"][...], halo[...])).astype(jnp.bfloat16)
    half = slots * FREQ
    three = mixed_dot(jnp.concatenate([upper[:half], upper[half:]], 1), held["cols"][...])
    first = lax.broadcasted_iota(jnp.int32, (FREQ, 128), 1) < 64
    own = jnp.where(first, three[:FREQ, :128], three[FREQ:, :128])
    out_msg[0] = jnp.where(first, three[:FREQ, 128:], pltpu.roll(three[FREQ:, 128:], 64, 1))
    out_msg[1] = jnp.where(first, pltpu.roll(three[:FREQ, 128:], 64, 1), three[FREQ:, 128:])
    sideways = []
    for n, dx in enumerate((-1, 1)):
        there, device = at.near(0, dx)
        copy = push(out_msg.at[n], side.at[n], side_send.at[n], side_recv.at[n], device)
        sideways.append((there, copy))
        pl.when(there)(copy.start)
    for n, (there, copy) in enumerate(sideways):
        source, _ = at.near(0, 1 if n == 0 else -1)
        pl.when(source)(copy.wait_recv)

        @pl.when(jnp.logical_not(source))
        def _():
            side[n] = jnp.zeros((FREQ, 128), jnp.float32)

    for name in COPIED[4:]:
        copies[name].wait()
    flags = [occ_ref[slot] for slot in range(slots)]
    total = spectrum_gradients(
        own + side[0] + side[1], flags, held["target"], kern_ref, root_ref, {n: held[n] for n in NAMES}, sens_ref
    )
    full[...] = total
    sent = []
    for n, offset in enumerate(NEAR):
        there, device = at.near(*offset)
        copy = push(full, near.at[n], near_send.at[n], near_recv.at[n], device)
        sent.append((there, copy))
        pl.when(there)(copy.start)
    for n, (dy, dx) in enumerate(NEAR):
        source, _ = at.near(-dy, -dx)
        pl.when(source)(sent[n][1].wait_recv)

        @pl.when(jnp.logical_not(source))
        def _():
            near[n] = jnp.zeros((FREQ, 128), jnp.float32)

    def product(dx, table):
        get = lambda dy: total if (dy, dx) == (0, 0) else near[NEAR.index((-dy, -dx))]
        upper, middle, lower = get(-1), get(0), get(1)
        stack = [
            jnp.where(first, 0.0, upper), jnp.where(first, middle, 0.0),
            jnp.where(first, 0.0, middle), jnp.where(first, lower, 0.0),
        ]
        high, low = two_parts(jnp.concatenate(stack, 0))
        return mixed_dot(high, table) + mixed_dot(low, table)

    own = product(0, held["own"][...])
    left = product(-1, held["beside"][0])
    right = product(1, held["beside"][1])
    for part in range(2):
        value = own[:, part * TILE : (part + 1) * TILE]
        span = slice(part * 128, part * 128 + 128)
        value = jnp.concatenate(
            [value[:, :128] + left[:, span], value[:, 128:-128], value[:, -128:] + right[:, span]], 1
        ).astype(jnp.bfloat16)
        for tile in range(slots + 2):
            low_ref[(2 * tile + part) * FREQ : (2 * tile + part + 1) * FREQ, :] = value[
                tile * FREQ : (tile + 1) * FREQ
            ]
    for there, copy in vertical + sideways + sent:
        pl.when(there)(copy.wait_send)


def whole_call(mask_field, target_field, occ, kernels, root, bands, size, slots):
    arrays = dict(zip(NAMES, grid_tables()))
    arrays["row_table"], arrays["edge"], arrays["cols"] = exchange_tables(slots)
    arrays["own"], arrays["beside"] = lowering_tables()
    arrays = {name: jnp.asarray(a) for name, a in arrays.items()}
    arrays["mask"], arrays["target"] = mask_field, target_field
    given = [arrays[name] for name in COPIED]
    dma = pltpu.SemaphoreType.DMA
    smem, hbm = pl.BlockSpec(memory_space=pltpu.SMEM), pl.BlockSpec(memory_space=pl.ANY)
    return pl.pallas_call(
        lambda *refs: whole(bands, size, slots, None, *refs),
        out_shape=jax.ShapeDtypeStruct(((slots + 2) * 2 * FREQ, TILE), jnp.bfloat16),
        in_specs=[smem, smem, VMEM] + [hbm] * len(given),
        out_specs=VMEM,
        scratch_shapes=[pltpu.VMEM(a.shape, a.dtype) for a in given]
        + [
            pltpu.VMEM((TILE, slots * TILE), jnp.bfloat16),
            pltpu.VMEM((2 * AMBIT, TILE), jnp.bfloat16),
            pltpu.VMEM((2, FREQ, 128), jnp.float32),
            pltpu.VMEM((2, FREQ, 128), jnp.float32),
            pltpu.VMEM((FREQ, 128), jnp.float32),
            pltpu.VMEM((len(NEAR), FREQ, 128), jnp.float32),
            dma((len(given),)),
            dma((2,)), dma((2,)), dma((2,)), dma((2,)), dma((len(NEAR),)), dma((len(NEAR),)),
        ],
        compiler_params=pltpu.CompilerParams(
            collective_id=0, has_side_effects=True, vmem_limit_bytes=52 * 1024 * 1024
        ),
    )(root, occ, kernels, *given)


def finish_call(lowered, mask_field, slots):
    table = jnp.asarray(np.ascontiguousarray(spread(slots).T))
    height, width = mask_field.shape
    rows = 128
    steps = height // rows

    def finish(table_ref, low_ref, mask_ref, out_ref, held, sems):
        copies = []
        for step in range(steps):
            span = pl.ds(step * rows, rows)
            values = mask_ref[span, :].astype(jnp.float32)
            penalty = GAMMA * 4.0 * values * (values * values - 1.0)
            held[span, :] = mixed_dot(table_ref[span, :], low_ref[...]) + penalty
            copies.append(pltpu.make_async_copy(held.at[span], out_ref.at[span], sems.at[step]))
            copies[-1].start()
        for copy in copies:
            copy.wait()

    return pl.pallas_call(
        finish,
        out_shape=jax.ShapeDtypeStruct((height, width), jnp.float32),
        in_specs=[VMEM, VMEM, VMEM],
        out_specs=pl.BlockSpec(memory_space=pl.ANY),
        scratch_shapes=[pltpu.VMEM((height, width), jnp.float32), pltpu.SemaphoreType.DMA((steps,))],
        compiler_params=pltpu.CompilerParams(vmem_limit_bytes=16 * 1024 * 1024),
    )(table, lowered, mask_field)


def on_device(mask_field, target_field, occupancy, kernels, weights):
    slots = mask_field.shape[0] // TILE
    bands, size = lax.axis_size("own"), lax.axis_size("img")
    assert slots == 2
    band, column = lax.axis_index("own"), lax.axis_index("img")
    occ = lax.dynamic_slice(occupancy, (band * slots, column), (slots, 1))[:, 0]
    lowered = whole_call(mask_field, target_field, occ, kernels, jnp.sqrt(weights), bands, size, slots)
    return finish_call(lowered, mask_field, slots)


def solution(mesh):
    return jax.shard_map(
        on_device,
        mesh=mesh,
        in_specs=(P("own", "img"), P("own", "img"), P(), P(), P()),
        out_specs=P("own", "img"),
        check_vma=False,
    )
```

time: 108 us -> 34.1 us (0.32)
  the two profiles are of different devices: /device:TPU:11 before, /device:TPU:4 now
where the time goes in v1:
time: 34.1 us; the launch traced here: 33.6 us
  Pallas kernels  23.2 us (68%)
  local copies, waits for them, and re-layouts  10.3 us (30%)
    pallas_call x1, Pallas kernels, whole_call(): pl.pallas_call(lambda *refs: whole(bands, size, slots, None, *refs), out_...  21.6 us
    unnamed x26, local copies, waits for them, and re-layouts  9.5 us
    pallas_call x1, Pallas kernels, finish_call(): pl.pallas_call(finish, out_shape=jax.ShapeDtypeStruct((height, width), jn...  1.6 us

profile of v1, /device:TPU:4, one launch (start us, length us, event | category | flops | bytes accessed | tf_op | source)
XLA Modules:
  0.0 33.6 jit_solution(17594330153906112761)
XLA Ops:
  0.0 0.0 copy-start
  0.0 0.7 %copy-done = s32[8,8]{1,0:T(8,128)S(1)} copy-done((s32[8,8]{1,0:T(8,128)S(1)}, s32[8,8]{1,0:T(8,128)}, u32[]{:S(2)}) %copy-start) | copy-done | bytes 280
  0.7 0.2 dynamic-slice_reduce_fusion.refs_1_
  0.9 0.7 %sqrt.3.refs_0_ = f32[24]{0:T(128)S(1)} sqrt(f32[24]{0:T(128)} %param.23) | non-fusion elementwise | bytes 192 | tf_op jit(solution)/shard_map/sqrt | solution.py:382
  1.5 0.0 copy-start.3
  1.5 1.0 %copy-done.3 = bf16[128,1024]{1,0:T(8,128)(2,1)S(1)} copy-done((bf16[128,1024]{1,0:T(8,128)(2,1)S(1)}, bf16[128,1024]{1,0:T(8,128)(2,1)}, u32[]{:S(2)}) %copy-start.3) | copy-done | bytes 262168
  2.5 0.0 copy-start.4
  2.5 0.9 %copy-done.4 = bf16[512,256]{1,0:T(8,128)(2,1)S(1)} copy-done((bf16[512,256]{1,0:T(8,128)(2,1)S(1)}, bf16[512,256]{1,0:T(8,128)(2,1)}, u32[]{:S(2)}) %copy-start.4) | copy-done | bytes 262168
  3.4 0.0 copy-start.5
  3.4 0.9 %copy-done.5 = bf16[256,512]{1,0:T(8,128)(2,1)S(1)} copy-done((bf16[256,512]{1,0:T(8,128)(2,1)S(1)}, bf16[256,512]{1,0:T(8,128)(2,1)}, u32[]{:S(2)}) %copy-start.5) | copy-done | bytes 262168
  4.4 0.0 copy-start.6
  4.4 0.9 %copy-done.6 = bf16[512,256]{1,0:T(8,128)(2,1)S(1)} copy-done((bf16[512,256]{1,0:T(8,128)(2,1)S(1)}, bf16[512,256]{1,0:T(8,128)(2,1)}, u32[]{:S(2)}) %copy-start.6) | copy-done | bytes 262168
  5.3 0.0 copy-start.7
  5.3 0.9 %copy-done.7 = bf16[384,256]{1,0:T(8,128)(2,1)S(1)} copy-done((bf16[384,256]{1,0:T(8,128)(2,1)S(1)}, bf16[384,256]{1,0:T(8,128)(2,1)}, u32[]{:S(2)}) %copy-start.7) | copy-done | bytes 196632
  6.3 0.0 copy-start.8
  6.3 0.9 %copy-done.8 = bf16[2,128,256]{2,1,0:T(8,128)(2,1)S(1)} copy-done((bf16[2,128,256]{2,1,0:T(8,128)(2,1)S(1)}, bf16[2,128,256]{2,1,0:T(8,128)(2,1)}, u32[]{:S(2)}) %copy-start.8) | copy-done | bytes 131096
  7.2 0.0 copy-start.9
  7.2 0.9 %copy-done.9 = bf16[128,512]{1,0:T(8,128)(2,1)S(1)} copy-done((bf16[128,512]{1,0:T(8,128)(2,1)S(1)}, bf16[128,512]{1,0:T(8,128)(2,1)}, u32[]{:S(2)}) %copy-start.9) | copy-done | bytes 131096
  8.1 0.0 copy-start.10
  8.1 0.8 %copy-done.10 = bf16[128,128]{1,0:T(8,128)(2,1)S(1)} copy-done((bf16[128,128]{1,0:T(8,128)(2,1)S(1)}, bf16[128,128]{1,0:T(8,128)(2,1)}, u32[]{:S(2)}) %copy-start.10) | copy-done | bytes 32792
  8.8 0.0 copy-start.11
  8.8 0.8 %copy-done.11 = bf16[64,192]{1,0:T(8,128)(2,1)S(1)} copy-done((bf16[64,192]{1,0:T(8,128)(2,1)S(1)}, bf16[64,192]{1,0:T(8,128)(2,1)}, u32[]{:S(2)}) %copy-start.11) | copy-done | bytes 24600
  9.6 0.0 copy-start.12
  9.6 0.8 %copy-done.12 = bf16[64,192]{1,0:T(8,128)(2,1)S(1)} copy-done((bf16[64,192]{1,0:T(8,128)(2,1)S(1)}, bf16[64,192]{1,0:T(8,128)(2,1)}, u32[]{:S(2)}) %copy-start.12) | copy-done | bytes 24600
  10.4 0.0 copy-start.1
  10.4 0.0 copy-start.2
  10.4 21.6 %shard_map.181.low_ref = bf16[256,512]{1,0:T(8,128)(2,1)S(1)} custom-call(f32[24]{0:T(128)S(1)} %sqrt.3.refs_0_, s32[2]{0:T(128)S(1)} %dynamic-slice_reduce_fusion.refs_1_, f32[2,24,32,32]{3,2,1,0:T(8,128)} %refs_2_.1, bf16[1024,512]{1,0:T(8,128)(2,1)} %mask_ref.1, bf16[128,1024]{1,0:T(8,128)(2,1)S(1)} %copy-done.3, bf16[128,128]{1,0:T(8,128)(2,1)S(1)} %copy-done.10, ...), custom_call_target="tpu_custom_call" | custom-call | tf_op jit(solution)/shard_map/pallas_call | solution.py:326
  32.0 0.0 copy-done.1
  32.0 0.0 copy-done.2
  32.0 1.6 %shard_map.182 = f32[1024,512]{1,0:T(8,128)} custom-call(bf16[1024,256]{1,0:T(8,128)(2,1)S(1)} %copy-done.2, bf16[256,512]{1,0:T(8,128)(2,1)S(1)} %shard_map.181.low_ref, bf16[1024,512]{1,0:T(8,128)(2,1)S(1)} %copy-done.1), custom_call_target="tpu_custom_call" | custom-call | tf_op jit(solution)/shard_map/pallas_call | solution.py:366
Async XLA Ops:
  0.0 0.7 %copy-start = (s32[8,8]{1,0:T(8,128)S(1)}, s32[8,8]{1,0:T(8,128)}, u32[]{:S(2)}) copy-start(s32[8,8]{1,0:T(8,128)} %param.21) | copy-start | bytes 772
  1.5 1.0 %copy-start.3 = (bf16[128,1024]{1,0:T(8,128)(2,1)S(1)}, bf16[128,1024]{1,0:T(8,128)(2,1)}, u32[]{:S(2)}) copy-start(bf16[128,1024]{1,0:T(8,128)(2,1)} %constant.50.clone.refs_4_) | copy-start | bytes 786436
  2.5 0.9 %copy-start.4 = (bf16[512,256]{1,0:T(8,128)(2,1)S(1)}, bf16[512,256]{1,0:T(8,128)(2,1)}, u32[]{:S(2)}) copy-start(bf16[512,256]{1,0:T(8,128)(2,1)} %constant.49.clone.refs_13_) | copy-start | bytes 786436
  3.4 0.9 %copy-start.5 = (bf16[256,512]{1,0:T(8,128)(2,1)S(1)}, bf16[256,512]{1,0:T(8,128)(2,1)}, u32[]{:S(2)}) copy-start(bf16[256,512]{1,0:T(8,128)(2,1)} %constant.47.clone.refs_9_) | copy-start | bytes 786436
  4.4 0.9 %copy-start.6 = (bf16[512,256]{1,0:T(8,128)(2,1)S(1)}, bf16[512,256]{1,0:T(8,128)(2,1)}, u32[]{:S(2)}) copy-start(bf16[512,256]{1,0:T(8,128)(2,1)} %constant.46.clone.refs_10_) | copy-start | bytes 786436
  5.3 0.9 %copy-start.7 = (bf16[384,256]{1,0:T(8,128)(2,1)S(1)}, bf16[384,256]{1,0:T(8,128)(2,1)}, u32[]{:S(2)}) copy-start(bf16[384,256]{1,0:T(8,128)(2,1)} %constant.42.clone.refs_7_) | copy-start | bytes 589828
  6.3 0.9 %copy-start.8 = (bf16[2,128,256]{2,1,0:T(8,128)(2,1)S(1)}, bf16[2,128,256]{2,1,0:T(8,128)(2,1)}, u32[]{:S(2)}) copy-start(bf16[2,128,256]{2,1,0:T(8,128)(2,1)} %constant.54.clone.refs_17_) | copy-start | bytes 393220
  7.2 0.9 %copy-start.9 = (bf16[128,512]{1,0:T(8,128)(2,1)S(1)}, bf16[128,512]{1,0:T(8,128)(2,1)}, u32[]{:S(2)}) copy-start(bf16[128,512]{1,0:T(8,128)(2,1)} %constant.48.clone.refs_12_) | copy-start | bytes 393220
  8.1 0.8 %copy-start.10 = (bf16[128,128]{1,0:T(8,128)(2,1)S(1)}, bf16[128,128]{1,0:T(8,128)(2,1)}, u32[]{:S(2)}) copy-start(bf16[128,128]{1,0:T(8,128)(2,1)} %constant.51.clone.refs_5_) | copy-start | bytes 98308
  8.8 0.8 %copy-start.11 = (bf16[64,192]{1,0:T(8,128)(2,1)S(1)}, bf16[64,192]{1,0:T(8,128)(2,1)}, u32[]{:S(2)}) copy-start(bf16[64,192]{1,0:T(8,128)(2,1)} %constant.44.clone.refs_14_) | copy-start | bytes 73732
  9.6 0.8 %copy-start.12 = (bf16[64,192]{1,0:T(8,128)(2,1)S(1)}, bf16[64,192]{1,0:T(8,128)(2,1)}, u32[]{:S(2)}) copy-start(bf16[64,192]{1,0:T(8,128)(2,1)} %constant.43.clone.refs_8_) | copy-start | bytes 73732
  10.4 21.6 %copy-start.1 = (bf16[1024,512]{1,0:T(8,128)(2,1)S(1)}, bf16[1024,512]{1,0:T(8,128)(2,1)}, u32[]{:S(2)}) copy-start(bf16[1024,512]{1,0:T(8,128)(2,1)} %mask_ref.1) | copy-start | bytes 3145732
  10.4 21.6 %copy-start.2 = (bf16[1024,256]{1,0:T(8,128)(2,1)S(1)}, bf16[1024,256]{1,0:T(8,128)(2,1)}, u32[]{:S(2)}) copy-start(bf16[1024,256]{1,0:T(8,128)(2,1)} %constant.55.clone.table_ref) | copy-start | bytes 1572868

commit v2 on v1

v2 whole, which is shorter than its diff:
```python
import math

import jax
import jax.numpy as jnp
import numpy as np
from jax import lax
from jax.experimental import pallas as pl
from jax.experimental.pallas import tpu as pltpu
from jax.sharding import PartitionSpec as P

TILE = 512
AMBIT = 64
FREQ = 32
KERNELS = 24
PAD = 640
STEEP = 2.0
THRESHOLD = 1.5
GAMMA = 0.25
VMEM_GRANT = 61 * 1024 * 1024
GRID = 64


def tables():
    freqs = np.arange(FREQ) - FREQ // 2
    turn = np.float32(2.0 * math.pi / PAD)
    phase = ((freqs[:, None] * np.arange(PAD)[None, :]) % PAD).astype(np.float32) * turn
    bf = lambda a: np.asarray(a, np.float32).astype(jnp.bfloat16)
    return (
        bf(np.cos(phase) / np.float32(math.sqrt(PAD))),
        bf(-np.sin(phase) / np.float32(math.sqrt(PAD))),
    )


FC, FS = tables()
FORWARD = np.concatenate([FC, FS], 0)


def spread(count):
    length = count * TILE
    out = np.zeros((count + 2, 2 * FREQ, length), jnp.bfloat16)
    for tile in range(-1, count + 1):
        start = tile * TILE - AMBIT
        low, high = max(start, 0), min(start + PAD, length)
        out[tile + 1, :, low:high] = FORWARD[:, low - start : high - start]
    return out.reshape(-1, length)


def two_tables(table):
    high = np.asarray(table).astype(jnp.bfloat16)
    return high, (table - high.astype(np.float64)).astype(jnp.bfloat16)


def grid_tables():
    freqs = np.arange(FREQ) - FREQ // 2
    turn = 2.0 * math.pi * (np.arange(GRID)[:, None] * freqs[None, :]) / GRID
    c, s = np.cos(turn) / math.sqrt(FREQ), np.sin(turn) / math.sqrt(FREQ)
    zero = np.zeros((2 * FREQ, 2 * GRID))
    one = np.block([[c.T, s.T], [-s.T, c.T]])
    there_high, there_low = two_tables(np.block([[one, zero], [zero, one]]))
    there = np.concatenate([there_high, there_low], 0)
    high, _ = two_tables(np.concatenate([c, s], 1))
    rows = np.concatenate([high, np.zeros_like(high)], 1)
    rows_back = np.concatenate([high.T, np.zeros_like(high)], 1)
    zero = np.zeros((2 * GRID, 2 * FREQ))
    parts = []
    for adj in (np.block([[c, -s], [s, c]]), np.block([[-s, -c], [c, -s]])):
        parts.append(np.block([[adj, zero], [zero, adj]]))
    back, _ = two_tables(np.concatenate(parts, 0))
    waves = np.arange(-(FREQ - 1), FREQ)
    apart = (np.arange(TILE) + AMBIT)[:, None] / PAD - np.arange(GRID)[None, :] / GRID
    fine = np.cos(2.0 * math.pi * apart[:, :, None] * waves).sum(-1) / GRID
    high, low = two_tables(fine)
    up = np.concatenate([high, high, low, np.zeros_like(low)], 1)
    down = np.concatenate([high.T, low.T], 0)
    down_cols = np.concatenate([high, high, low, low], 1)
    return there, rows, rows_back, back, up, np.ascontiguousarray(up.T), down, down_cols


def exchange_tables(slots):
    rows = spread(slots).reshape(slots + 2, 2, FREQ, -1).transpose(1, 0, 2, 3).reshape(2 * (slots + 2) * FREQ, -1)
    near = spread(1).reshape(3, 2, FREQ, TILE)
    cols = []
    for which in (1, 1, 0, 2):
        c, s = near[which].astype(np.float32)
        cols.append(np.block([[c.T, s.T], [-s.T, c.T]]))
    return rows, np.concatenate(cols, 1).astype(jnp.bfloat16)


def lowering_tables():
    near = spread(1).reshape(3, 2, FREQ, TILE).astype(np.float32)
    full = [np.block([[c, -s], [s, c]]) for c, s in near]
    cut = [np.block([[c, -s], [s, c]]) for c, s in (near[0][:, :, :128], near[2][:, :, -128:])]
    twice = lambda a: np.concatenate([a, a], 0).astype(jnp.bfloat16)
    return twice(full[1]), np.stack([twice(cut[0]), twice(cut[1])])


def mixed_dot(left, right):
    return jnp.dot(left, right, preferred_element_type=jnp.float32)


def two_parts(value):
    high = value.astype(jnp.bfloat16)
    return high, (value - high.astype(jnp.float32)).astype(jnp.bfloat16)


MESH = pl.DeviceIdType.MESH
VMEM = pl.BlockSpec(memory_space=pltpu.VMEM)
NEAR = [(dy, dx) for dy in (-1, 0, 1) for dx in (-1, 0, 1) if (dy, dx) != (0, 0)]


class Place:
    def __init__(self, bands, size):
        self.bands, self.size = bands, size
        self.band, self.column = lax.axis_index("own"), lax.axis_index("img")

    def near(self, dy, dx):
        row, col = self.band + dy, self.column + dx
        there = (row >= 0) & (row < self.bands) & (col >= 0) & (col < self.size)
        return there, (row, col)

    def greet(self):
        barrier = pltpu.get_barrier_semaphore()
        count = jnp.int32(0)
        for offset in NEAR:
            there, device = self.near(*offset)
            count = count + there.astype(jnp.int32)

            @pl.when(there)
            def _():
                pl.semaphore_signal(barrier, inc=1, device_id=device, device_id_type=MESH)

        return lambda: pl.semaphore_wait(barrier, count)


def push(src, dst, send, recv, device):
    return pltpu.make_async_remote_copy(
        src_ref=src, dst_ref=dst, send_sem=send, recv_sem=recv, device_id=device, device_id_type=MESH
    )


def swapped(value, lane):
    return jnp.where(lane % 64 < 32, pltpu.roll(value, 96, 1), pltpu.roll(value, 32, 1))


def spectrum_gradients(m, flags, wanted, kr_ref, ki_ref, t, sens_ref):
    lane = lax.broadcasted_iota(jnp.int32, (FREQ, 128), 1)
    sign = jnp.where(lane % 64 < 32, -1.0, 1.0)
    n = sign * swapped(m, lane)
    parts = []
    for k in range(KERNELS):
        kr, ki = kr_ref[k], ki_ref[k]
        parts += [kr * m + ki * n, kr * n - ki * m]
    high = jnp.concatenate(parts, 0).astype(jnp.bfloat16)
    half = mixed_dot(jnp.concatenate([high, high], 1), t["there"][...]).astype(jnp.bfloat16)
    rows_table, rows_back = t["rows"][:, : 2 * FREQ], t["rows_back"][:, : 2 * FREQ]
    fields = []
    total = jnp.zeros((GRID, 256), jnp.float32)
    for k in range(KERNELS):
        field = mixed_dot(rows_table, half[k * 64 : (k + 1) * 64])
        fields.append(field)
        total = total + field * field
    coarse = jnp.concatenate([total[:, :128], total[:, 128:]], 0)
    coarse = coarse + pltpu.roll(coarse, 64, 1)
    high, low = two_parts(coarse)
    first = lax.broadcasted_iota(jnp.int32, (2 * GRID, 128), 1) < 64
    zero = jnp.zeros((2 * GRID, 128), jnp.float32)
    high32, low32 = high.astype(jnp.float32), low.astype(jnp.float32)
    lhs = jnp.concatenate([jnp.where(first, high32, low32), jnp.where(first, high32, zero)], 1).astype(jnp.bfloat16)
    across = mixed_dot(lhs, t["up_t"][...])
    high, low = two_parts(across)
    rows = 128
    for slot in range(2):
        at = slice(slot * GRID, (slot + 1) * GRID)
        rhs = jnp.concatenate([high[at], low[at], high[at], jnp.zeros((GRID, TILE), jnp.bfloat16)], 0)
        for start in range(0, TILE, rows):
            intensity = mixed_dot(t["up"][start : start + rows, :], rhs)
            bend = jnp.tanh((0.5 * STEEP) * (intensity - THRESHOLD))
            goal = wanted[slot * TILE + start : slot * TILE + start + rows, :].astype(jnp.float32)
            sens = (0.5 * STEEP) * (1.0 + bend - 2.0 * goal) * (1.0 - bend * bend)
            sens_ref[start : start + rows, slot * TILE : (slot + 1) * TILE] = sens.astype(jnp.bfloat16)
    folded = mixed_dot(t["down"][...], sens_ref[...])
    folded = folded[:GRID] + folded[GRID:]
    high, low = two_parts(jnp.concatenate([folded[:, :TILE], folded[:, TILE:]], 0))
    grid = mixed_dot(jnp.concatenate([high, low], 0), t["down_cols"][...])
    grid = grid[:128, :128] + grid[:128, 128:] + grid[128:, :128]
    weight = jnp.concatenate([grid[:GRID], grid[GRID:]], 1)
    tops, bottoms = [], []
    for k in range(KERNELS):
        pulled = mixed_dot(rows_back, (fields[k] * weight).astype(jnp.bfloat16))
        tops.append(pulled[:FREQ])
        bottoms.append(pulled[FREQ:])
    pulled = jnp.concatenate([jnp.concatenate(tops, 0), jnp.concatenate(bottoms, 0)], 1)
    back = mixed_dot(pulled.astype(jnp.bfloat16), t["back"][...])
    sum_r = jnp.zeros((FREQ, 128), jnp.float32)
    sum_i = jnp.zeros((FREQ, 128), jnp.float32)
    for k in range(KERNELS):
        z = back[k * FREQ : (k + 1) * FREQ]
        sum_r = sum_r + kr_ref[k] * z
        sum_i = sum_i + ki_ref[k] * z
    grad = sum_r - sign * swapped(sum_i, lane)
    return jnp.where(jnp.where(lane < 64, flags[0], flags[1]) > 0, grad, 0.0)


def packed(arrays):
    pieces, places, top = [], [], 0
    for name, table in arrays.items():
        height, width = table.shape
        for left in range(0, width, 256):
            piece = table[:, left : left + 256]
            places.append((name, top, height, left, piece.shape[1]))
            pieces.append(np.pad(piece, ((0, 0), (0, 256 - piece.shape[1]))))
            top += height
    return np.concatenate(pieces, 0), places


def all_tables(slots):
    arrays = {}
    arrays["row_table"], arrays["cols"] = exchange_tables(slots)
    names = ["there", "rows", "rows_back", "back", "up", "up_t", "down", "down_cols"]
    grid = dict(zip(names, grid_tables()))
    for name in ("there", "rows", "up_t", "up", "down", "down_cols", "rows_back", "back"):
        arrays[name] = grid[name]
    arrays["own"], beside = lowering_tables()
    arrays["left"], arrays["right"] = beside
    return arrays


def whole(
    bands, size, slots, names, places, root_ref, occ_ref, kern_hbm, mask_hbm, targ_hbm, packed_hbm, low_ref, *refs
):
    count = len(names)
    held = dict(zip(names, refs[:count]))
    (kern_ref, mask_ref, targ_ref, kr_ref, ki_ref, sens_ref, out_msg, side, full, near, copy_sem, table_sem,
     side_send, side_recv, near_send, near_recv) = refs[count:]
    at = Place(bands, size)
    arrived = at.greet()
    copies = []
    for n, (src, dst) in enumerate(((mask_hbm, mask_ref), (kern_hbm, kern_ref), (targ_hbm, targ_ref))):
        copies.append(pltpu.make_async_copy(src, dst, copy_sem.at[n]))
    tables = []
    for n, (name, top, height, left, width) in enumerate(places):
        tables.append(
            pltpu.make_async_copy(
                packed_hbm.at[pl.ds(top, height), pl.ds(0, width)],
                held[name].at[:, pl.ds(left, width)],
                table_sem.at[n],
            )
        )
    early = [c for c, place in zip(tables, places) if place[0] in ("row_table", "cols")]
    late = [c for c, place in zip(tables, places) if place[0] not in ("row_table", "cols")]
    for copy in [copies[0]] + early + copies[1:] + late:
        copy.start()

    for copy in [copies[0]] + early:
        copy.wait()
    upper = mixed_dot(held["row_table"][...], mask_ref[...]).astype(jnp.bfloat16)
    half = (slots + 2) * FREQ
    three = mixed_dot(jnp.concatenate([upper[:half], upper[half:]], 1), held["cols"][...])
    first = lax.broadcasted_iota(jnp.int32, (FREQ, 128), 1) < 64

    def packed_part(dy, dx):
        def rows(tile):
            span = slice((tile + 1) * FREQ, (tile + 2) * FREQ)
            if dx == 0:
                return three[span, :128]
            value = three[span, 128:]
            turned = pltpu.roll(value, 64, 1)
            return jnp.where(first, value, turned) if dx < 0 else jnp.where(first, turned, value)

        if dy == 0:
            return jnp.where(first, rows(0), rows(1))
        return jnp.where(first, 0.0, rows(-1)) if dy < 0 else jnp.where(first, rows(slots), 0.0)

    spectrum = packed_part(0, 0)
    for n, offset in enumerate(NEAR):
        out_msg[n] = packed_part(*offset)
    arrived()

    def spread_out(sources, into, send, recv):
        sent = []
        for n, offset in enumerate(NEAR):
            there, device = at.near(*offset)
            copy = push(sources[n], into.at[n], send.at[n], recv.at[n], device)
            sent.append((there, copy))
            pl.when(there)(copy.start)
        return sent

    def take_in(sent, into):
        for n, (dy, dx) in enumerate(NEAR):
            source, _ = at.near(-dy, -dx)
            pl.when(source)(sent[n][1].wait_recv)

            @pl.when(jnp.logical_not(source))
            def _():
                into[n] = jnp.zeros((FREQ, 128), jnp.float32)

    parts_sent = spread_out([out_msg.at[n] for n in range(len(NEAR))], side, side_send, side_recv)
    copies[1].wait()
    for k in range(KERNELS):
        root = jnp.sqrt(jnp.full((1, 128), root_ref[k], jnp.float32))
        for part, ref in ((0, kr_ref), (1, ki_ref)):
            ref[k] = jnp.concatenate([kern_ref[part, k]] * 4, 1) * root
    for copy in copies[2:] + late:
        copy.wait()
    flags = [occ_ref[at.band * slots + slot, at.column] for slot in range(slots)]
    take_in(parts_sent, side)
    for n in range(len(NEAR)):
        spectrum = spectrum + side[n]
    total = spectrum_gradients(spectrum, flags, targ_ref, kr_ref, ki_ref, held, sens_ref)
    full[...] = total
    sent = spread_out([full] * len(NEAR), near, near_send, near_recv)
    take_in(sent, near)

    def product(dx, table):
        get = lambda dy: total if (dy, dx) == (0, 0) else near[NEAR.index((-dy, -dx))]
        upper, middle, lower = get(-1), get(0), get(1)
        stack = [
            jnp.where(first, 0.0, upper), jnp.where(first, middle, 0.0),
            jnp.where(first, 0.0, middle), jnp.where(first, lower, 0.0),
        ]
        high, low = two_parts(jnp.concatenate(stack, 0))
        return mixed_dot(high, table) + mixed_dot(low, table)

    own = product(0, held["own"][...])
    left = product(-1, held["left"][...])
    right = product(1, held["right"][...])
    for part in range(2):
        value = own[:, part * TILE : (part + 1) * TILE]
        span = slice(part * 128, part * 128 + 128)
        value = jnp.concatenate(
            [value[:, :128] + left[:, span], value[:, 128:-128], value[:, -128:] + right[:, span]], 1
        ).astype(jnp.bfloat16)
        for tile in range(slots + 2):
            low_ref[(2 * tile + part) * FREQ : (2 * tile + part + 1) * FREQ, :] = value[
                tile * FREQ : (tile + 1) * FREQ
            ]
    for there, copy in parts_sent + sent:
        pl.when(there)(copy.wait_send)


def whole_call(mask_field, target_field, occupancy, kernels, weights, bands, size, slots):
    arrays = all_tables(slots)
    tables, places = packed(arrays)
    dma = pltpu.SemaphoreType.DMA
    smem, hbm = pl.BlockSpec(memory_space=pltpu.SMEM), pl.BlockSpec(memory_space=pl.ANY)
    message = pltpu.VMEM((len(NEAR), FREQ, 128), jnp.float32)
    spectra = pltpu.VMEM((KERNELS, FREQ, 128), jnp.float32)
    return pl.pallas_call(
        lambda *refs: whole(bands, size, slots, list(arrays), places, *refs),
        out_shape=jax.ShapeDtypeStruct(((slots + 2) * 2 * FREQ, TILE), jnp.bfloat16),
        in_specs=[smem, smem, hbm, hbm, hbm, hbm],
        out_specs=VMEM,
        scratch_shapes=[pltpu.VMEM(a.shape, jnp.bfloat16) for a in arrays.values()]
        + [
            pltpu.VMEM(kernels.shape, kernels.dtype),
            pltpu.VMEM(mask_field.shape, mask_field.dtype),
            pltpu.VMEM(target_field.shape, target_field.dtype),
            spectra, spectra,
            pltpu.VMEM((TILE, slots * TILE), jnp.bfloat16),
            message, message,
            pltpu.VMEM((FREQ, 128), jnp.float32),
            message,
            dma((3,)), dma((len(places),)),
            dma((len(NEAR),)), dma((len(NEAR),)), dma((len(NEAR),)), dma((len(NEAR),)),
        ],
        compiler_params=pltpu.CompilerParams(
            collective_id=0, has_side_effects=True, vmem_limit_bytes=VMEM_GRANT
        ),
    )(weights, occupancy, kernels, mask_field, target_field, jnp.asarray(tables))


def finish_call(lowered, mask_field, slots):
    table = jnp.asarray(np.ascontiguousarray(spread(slots).T))
    height, width = mask_field.shape
    rows = 128
    steps = height // rows

    def finish(table_ref, low_ref, mask_ref, out_ref, held, sems):
        copies = []
        for step in range(steps):
            span = pl.ds(step * rows, rows)
            values = mask_ref[span, :].astype(jnp.float32)
            penalty = GAMMA * 4.0 * values * (values * values - 1.0)
            held[span, :] = mixed_dot(table_ref[span, :], low_ref[...]) + penalty
            copies.append(pltpu.make_async_copy(held.at[span], out_ref.at[span], sems.at[step]))
            copies[-1].start()
        for copy in copies:
            copy.wait()

    return pl.pallas_call(
        finish,
        out_shape=jax.ShapeDtypeStruct((height, width), jnp.float32),
        in_specs=[VMEM, VMEM, VMEM],
        out_specs=pl.BlockSpec(memory_space=pl.ANY),
        scratch_shapes=[pltpu.VMEM((height, width), jnp.float32), pltpu.SemaphoreType.DMA((steps,))],
        compiler_params=pltpu.CompilerParams(vmem_limit_bytes=16 * 1024 * 1024),
    )(table, lowered, mask_field)


def on_device(mask_field, target_field, occupancy, kernels, weights):
    slots = mask_field.shape[0] // TILE
    bands, size = lax.axis_size("own"), lax.axis_size("img")
    assert slots == 2
    lowered = whole_call(mask_field, target_field, occupancy, kernels, weights, bands, size, slots)
    return finish_call(lowered, mask_field, slots)


def solution(mesh):
    return jax.shard_map(
        on_device,
        mesh=mesh,
        in_specs=(P("own", "img"), P("own", "img"), P(), P(), P()),
        out_specs=P("own", "img"),
        check_vma=False,
    )
```

time: 34.1 us -> 20.1 us (0.59)
  the two profiles are of different devices: /device:TPU:4 before, /device:TPU:1 now
where the time goes in v2:
time: 20.1 us; the launch traced here: 19.9 us
  Pallas kernels  19 us (95%)
  local copies, waits for them, and re-layouts  0.95 us (5%)
    pallas_call x1, Pallas kernels, whole_call(): pl.pallas_call(lambda *refs: whole(bands, size, slots, list(arrays), plac...  17.4 us
    pallas_call x1, Pallas kernels, finish_call(): pl.pallas_call(finish, out_shape=jax.ShapeDtypeStruct((height, width), jn...  1.6 us
    unnamed x6, local copies, waits for them, and re-layouts  0.95 us

profile of v2, /device:TPU:1, one launch (start us, length us, event | category | flops | bytes accessed | tf_op | source)
XLA Modules:
  0.0 19.9 jit_solution(11667022853808806619)
XLA Ops:
  0.0 0.0 copy-start.2
  0.0 0.0 copy-start
  0.0 17.4 %shard_map.73.low_ref = bf16[256,512]{1,0:T(8,128)(2,1)} custom-call(f32[24]{0:T(128)} %refs_0_.1, s32[8,8]{1,0:T(8,128)} %refs_1_.1, f32[2,24,32,32]{3,2,1,0:T(8,128)} %refs_2_.1, bf16[1024,512]{1,0:T(8,128)(2,1)} %mask_ref.1, bf16[1024,512]{1,0:T(8,128)(2,1)} %refs_4_.1, bf16[5504,256]{1,0:T(8,128)(2,1)} %constant.4.clone.refs_5_), custom_call_target="tpu_custom_call" | custom-call | tf_op jit(solution)/shard_map/pallas_call | solution.py:348
  17.4 0.0 copy-done.2
  17.4 0.0 copy-done
  17.4 0.0 copy-start.1
  17.4 0.9 %copy-done.1 = bf16[256,512]{1,0:T(8,128)(2,1)S(1)} copy-done((bf16[256,512]{1,0:T(8,128)(2,1)S(1)}, bf16[256,512]{1,0:T(8,128)(2,1)}, u32[]{:S(2)}) %copy-start.1) | copy-done | bytes 262168
  18.3 1.6 %shard_map.74 = f32[1024,512]{1,0:T(8,128)} custom-call(bf16[1024,256]{1,0:T(8,128)(2,1)S(1)} %copy-done.2, bf16[256,512]{1,0:T(8,128)(2,1)S(1)} %copy-done.1, bf16[1024,512]{1,0:T(8,128)(2,1)S(1)} %copy-done), custom_call_target="tpu_custom_call" | custom-call | tf_op jit(solution)/shard_map/pallas_call | solution.py:390
Async XLA Ops:
  0.0 17.4 %copy-start.2 = (bf16[1024,256]{1,0:T(8,128)(2,1)S(1)}, bf16[1024,256]{1,0:T(8,128)(2,1)}, u32[]{:S(2)}) copy-start(bf16[1024,256]{1,0:T(8,128)(2,1)} %constant.5.clone.table_ref) | copy-start | bytes 1572868
  0.0 17.4 %copy-start = (bf16[1024,512]{1,0:T(8,128)(2,1)S(1)}, bf16[1024,512]{1,0:T(8,128)(2,1)}, u32[]{:S(2)}) copy-start(bf16[1024,512]{1,0:T(8,128)(2,1)} %mask_ref.1) | copy-start | bytes 3145732
  17.4 1.0 %copy-start.1 = (bf16[256,512]{1,0:T(8,128)(2,1)S(1)}, bf16[256,512]{1,0:T(8,128)(2,1)}, u32[]{:S(2)}) copy-start(bf16[256,512]{1,0:T(8,128)(2,1)} %shard_map.73.low_ref) | copy-start | bytes 786436

commit v3 on v2

--- a/solution.py
+++ b/solution.py
@@ -17,6 +17,7 @@
 THRESHOLD = 1.5
 GAMMA = 0.25
 VMEM_GRANT = 61 * 1024 * 1024
+PIECES = 4
 GRID = 64
 
 
@@ -168,7 +169,7 @@
     lhs = jnp.concatenate([jnp.where(first, high32, low32), jnp.where(first, high32, zero)], 1).astype(jnp.bfloat16)
     across = mixed_dot(lhs, t["up_t"][...])
     high, low = two_parts(across)
-    rows = 128
+    rows = 256
     for slot in range(2):
         at = slice(slot * GRID, (slot + 1) * GRID)
         rhs = jnp.concatenate([high[at], low[at], high[at], jnp.zeros((GRID, TILE), jnp.bfloat16)], 0)
@@ -226,17 +227,23 @@
 
 
 def whole(
-    bands, size, slots, names, places, root_ref, occ_ref, kern_hbm, mask_hbm, targ_hbm, packed_hbm, low_ref, *refs
+    bands, size, slots, names, places, root_hbm, occ_hbm, kern_hbm, mask_hbm, targ_hbm, packed_hbm, low_ref, *refs
 ):
     count = len(names)
     held = dict(zip(names, refs[:count]))
-    (kern_ref, mask_ref, targ_ref, kr_ref, ki_ref, sens_ref, out_msg, side, full, near, copy_sem, table_sem,
+    (root_ref, occ_ref, kern_ref, mask_ref, targ_ref, kr_ref, ki_ref, sens_ref, out_msg, side, full, near, copy_sem, table_sem,
      side_send, side_recv, near_send, near_recv) = refs[count:]
     at = Place(bands, size)
     arrived = at.greet()
     copies = []
-    for n, (src, dst) in enumerate(((mask_hbm, mask_ref), (kern_hbm, kern_ref), (targ_hbm, targ_ref))):
+    pairs = [(root_hbm, root_ref), (occ_hbm, occ_ref), (kern_hbm, kern_ref), (targ_hbm, targ_ref)]
+    piece = slots * TILE // PIECES
+    for n in range(PIECES):
+        span = pl.ds(n * piece, piece)
+        pairs.append((mask_hbm.at[span], mask_ref.at[span]))
+    for n, (src, dst) in enumerate(pairs):
         copies.append(pltpu.make_async_copy(src, dst, copy_sem.at[n]))
+    mask_copies, copies = copies[4:], copies[:4]
     tables = []
     for n, (name, top, height, left, width) in enumerate(places):
         tables.append(
@@ -248,10 +255,10 @@
         )
     early = [c for c, place in zip(tables, places) if place[0] in ("row_table", "cols")]
     late = [c for c, place in zip(tables, places) if place[0] not in ("row_table", "cols")]
-    for copy in [copies[0]] + early + copies[1:] + late:
+    for copy in mask_copies + early + copies + late:
         copy.start()
 
-    for copy in [copies[0]] + early:
+    for copy in mask_copies + early:
         copy.wait()
     upper = mixed_dot(held["row_table"][...], mask_ref[...]).astype(jnp.bfloat16)
     half = (slots + 2) * FREQ
@@ -295,12 +302,13 @@
                 into[n] = jnp.zeros((FREQ, 128), jnp.float32)
 
     parts_sent = spread_out([out_msg.at[n] for n in range(len(NEAR))], side, side_send, side_recv)
-    copies[1].wait()
+    for copy in copies[:3]:
+        copy.wait()
     for k in range(KERNELS):
         root = jnp.sqrt(jnp.full((1, 128), root_ref[k], jnp.float32))
         for part, ref in ((0, kr_ref), (1, ki_ref)):
             ref[k] = jnp.concatenate([kern_ref[part, k]] * 4, 1) * root
-    for copy in copies[2:] + late:
+    for copy in copies[3:] + late:
         copy.wait()
     flags = [occ_ref[at.band * slots + slot, at.column] for slot in range(slots)]
     take_in(parts_sent, side)
@@ -309,21 +317,28 @@
     total = spectrum_gradients(spectrum, flags, targ_ref, kr_ref, ki_ref, held, sens_ref)
     full[...] = total
     sent = spread_out([full] * len(NEAR), near, near_send, near_recv)
+
+    def product(stack, table):
+        high, low = two_parts(jnp.concatenate(stack, 0))
+        table = table[...]
+        return mixed_dot(jnp.concatenate([high, low], 1), jnp.concatenate([table, table], 0))
+
+    def halves(value):
+        return [jnp.where(first, value, 0.0), jnp.where(first, 0.0, value)]
+
+    middle = product(halves(total), held["own"])
     take_in(sent, near)
 
-    def product(dx, table):
-        get = lambda dy: total if (dy, dx) == (0, 0) else near[NEAR.index((-dy, -dx))]
-        upper, middle, lower = get(-1), get(0), get(1)
-        stack = [
-            jnp.where(first, 0.0, upper), jnp.where(first, middle, 0.0),
-            jnp.where(first, 0.0, middle), jnp.where(first, lower, 0.0),
-        ]
-        high, low = two_parts(jnp.concatenate(stack, 0))
-        return mixed_dot(high, table) + mixed_dot(low, table)
-
-    own = product(0, held["own"][...])
-    left = product(-1, held["left"][...])
-    right = product(1, held["right"][...])
+    def get(dy, dx):
+        return near[NEAR.index((-dy, -dx))]
+
+    def beside(dx, table):
+        outer = [jnp.where(first, 0.0, get(-1, dx)), jnp.where(first, get(1, dx), 0.0)]
+        return product([outer[0]] + halves(get(0, dx)) + [outer[1]], table)
+
+    outer = product([jnp.where(first, 0.0, get(-1, 0)), jnp.where(first, get(1, 0), 0.0)], held["own"])
+    left, right = beside(-1, held["left"]), beside(1, held["right"])
+    own = jnp.concatenate([outer[:FREQ], middle, outer[FREQ:]], 0)
     for part in range(2):
         value = own[:, part * TILE : (part + 1) * TILE]
         span = slice(part * 128, part * 128 + 128)
@@ -342,16 +357,18 @@
     arrays = all_tables(slots)
     tables, places = packed(arrays)
     dma = pltpu.SemaphoreType.DMA
-    smem, hbm = pl.BlockSpec(memory_space=pltpu.SMEM), pl.BlockSpec(memory_space=pl.ANY)
+    hbm = pl.BlockSpec(memory_space=pl.ANY)
     message = pltpu.VMEM((len(NEAR), FREQ, 128), jnp.float32)
     spectra = pltpu.VMEM((KERNELS, FREQ, 128), jnp.float32)
     return pl.pallas_call(
         lambda *refs: whole(bands, size, slots, list(arrays), places, *refs),
         out_shape=jax.ShapeDtypeStruct(((slots + 2) * 2 * FREQ, TILE), jnp.bfloat16),
-        in_specs=[smem, smem, hbm, hbm, hbm, hbm],
+        in_specs=[hbm] * 6,
         out_specs=VMEM,
         scratch_shapes=[pltpu.VMEM(a.shape, jnp.bfloat16) for a in arrays.values()]
         + [
+            pltpu.SMEM(weights.shape, weights.dtype),
+            pltpu.SMEM(occupancy.shape, occupancy.dtype),
             pltpu.VMEM(kernels.shape, kernels.dtype),
             pltpu.VMEM(mask_field.shape, mask_field.dtype),
             pltpu.VMEM(target_field.shape, target_field.dtype),
@@ -360,7 +377,7 @@
             message, message,
             pltpu.VMEM((FREQ, 128), jnp.float32),
             message,
-            dma((3,)), dma((len(places),)),
+            dma((4 + PIECES,)), dma((len(places),)),
             dma((len(NEAR),)), dma((len(NEAR),)), dma((len(NEAR),)), dma((len(NEAR),)),
         ],
         compiler_params=pltpu.CompilerParams(
@@ -372,16 +389,19 @@
 def finish_call(lowered, mask_field, slots):
     table = jnp.asarray(np.ascontiguousarray(spread(slots).T))
     height, width = mask_field.shape
-    rows = 128
+    rows = 256
     steps = height // rows
 
-    def finish(table_ref, low_ref, mask_ref, out_ref, held, sems):
+    def finish(table_ref, low_hbm, mask_ref, out_ref, low_ref, held, low_sem, sems):
+        fetch = pltpu.make_async_copy(low_hbm, low_ref, low_sem)
+        fetch.start()
+        values = mask_ref[...].astype(jnp.float32)
+        held[...] = GAMMA * 4.0 * values * (values * values - 1.0)
+        fetch.wait()
         copies = []
         for step in range(steps):
             span = pl.ds(step * rows, rows)
-            values = mask_ref[span, :].astype(jnp.float32)
-            penalty = GAMMA * 4.0 * values * (values * values - 1.0)
-            held[span, :] = mixed_dot(table_ref[span, :], low_ref[...]) + penalty
+            held[span, :] = held[span, :] + mixed_dot(table_ref[span, :], low_ref[...])
             copies.append(pltpu.make_async_copy(held.at[span], out_ref.at[span], sems.at[step]))
             copies[-1].start()
         for copy in copies:
@@ -390,10 +410,15 @@
     return pl.pallas_call(
         finish,
         out_shape=jax.ShapeDtypeStruct((height, width), jnp.float32),
-        in_specs=[VMEM, VMEM, VMEM],
+        in_specs=[VMEM, pl.BlockSpec(memory_space=pl.ANY), VMEM],
         out_specs=pl.BlockSpec(memory_space=pl.ANY),
-        scratch_shapes=[pltpu.VMEM((height, width), jnp.float32), pltpu.SemaphoreType.DMA((steps,))],
-        compiler_params=pltpu.CompilerParams(vmem_limit_bytes=16 * 1024 * 1024),
+        scratch_shapes=[
+            pltpu.VMEM(lowered.shape, lowered.dtype),
+            pltpu.VMEM((height, width), jnp.float32),
+            pltpu.SemaphoreType.DMA,
+            pltpu.SemaphoreType.DMA((steps,)),
+        ],
+        compiler_params=pltpu.CompilerParams(vmem_limit_bytes=VMEM_GRANT),
     )(table, lowered, mask_field)
 
 

time: 20.1 us -> 20 us (level)
  local copies, waits for them, and re-layouts: 0.95 us -> 0 us
  Pallas kernels: 19 us -> 19.9 us
    pallas_call x1, Pallas kernels: 1.6 us -> 3.93 us  [finish_call(): pl.pallas_call(finish, out_shape=jax.ShapeDtypeStruct((height, width), jn...]
    pallas_call x1, Pallas kernels: 17.4 us -> 15.9 us  [whole_call(): pl.pallas_call(lambda *refs: whole(bands, size, slots, list(arrays), plac...]
    unnamed x6 -> x0, local copies, waits for them, and re-layouts: 0.95 us -> none
where the time goes in v3:
time: 20 us; the launch traced here: 19.9 us
  Pallas kernels  19.9 us (99%)
    pallas_call x1, Pallas kernels, whole_call(): pl.pallas_call(lambda *refs: whole(bands, size, slots, list(arrays), plac...  15.9 us
    pallas_call x1, Pallas kernels, finish_call(): pl.pallas_call(finish, out_shape=jax.ShapeDtypeStruct((height, width), jn...  3.93 us

profile of v3, /device:TPU:1, one launch (start us, length us, event | category | flops | bytes accessed | tf_op | source)
XLA Modules:
  0.0 19.9 jit_solution(1430772101515676926)
XLA Ops:
  0.0 15.9 %shard_map.73.low_hbm = bf16[256,512]{1,0:T(8,128)(2,1)} custom-call(f32[24]{0:T(128)} %refs_0_.1, s32[8,8]{1,0:T(8,128)} %refs_1_.1, f32[2,24,32,32]{3,2,1,0:T(8,128)} %refs_2_.1, bf16[1024,512]{1,0:T(8,128)(2,1)} %mask_ref.1, bf16[1024,512]{1,0:T(8,128)(2,1)} %refs_4_.1, bf16[5504,256]{1,0:T(8,128)(2,1)} %constant.4.clone.refs_5_), custom_call_target="tpu_custom_call" | custom-call | tf_op jit(solution)/shard_map/pallas_call | solution.py:363
  15.9 3.9 %shard_map.74 = f32[1024,512]{1,0:T(8,128)} custom-call(bf16[1024,256]{1,0:T(8,128)(2,1)} %constant.5.clone.table_ref, bf16[256,512]{1,0:T(8,128)(2,1)} %shard_map.73.low_hbm, bf16[1024,512]{1,0:T(8,128)(2,1)} %mask_ref.1), custom_call_target="tpu_custom_call" | custom-call | tf_op jit(solution)/shard_map/pallas_call | solution.py:410

commit v4 on v3

--- a/solution.py
+++ b/solution.py
@@ -16,7 +16,7 @@
 STEEP = 2.0
 THRESHOLD = 1.5
 GAMMA = 0.25
-VMEM_GRANT = 61 * 1024 * 1024
+VMEM_GRANT = 107 * 512 * 1024
 PIECES = 4
 GRID = 64
 
@@ -227,23 +227,23 @@
 
 
 def whole(
-    bands, size, slots, names, places, root_hbm, occ_hbm, kern_hbm, mask_hbm, targ_hbm, packed_hbm, low_ref, *refs
+    bands, size, slots, names, places, root_ref, occ_ref, kern_hbm, mask_hbm, targ_hbm, packed_hbm, low_ref, *refs
 ):
     count = len(names)
     held = dict(zip(names, refs[:count]))
-    (root_ref, occ_ref, kern_ref, mask_ref, targ_ref, kr_ref, ki_ref, sens_ref, out_msg, side, full, near, copy_sem, table_sem,
+    (kern_ref, mask_ref, targ_ref, kr_ref, ki_ref, sens_ref, out_msg, side, full, near, copy_sem, table_sem,
      side_send, side_recv, near_send, near_recv) = refs[count:]
     at = Place(bands, size)
     arrived = at.greet()
     copies = []
-    pairs = [(root_hbm, root_ref), (occ_hbm, occ_ref), (kern_hbm, kern_ref), (targ_hbm, targ_ref)]
+    pairs = [(kern_hbm, kern_ref), (targ_hbm, targ_ref)]
     piece = slots * TILE // PIECES
     for n in range(PIECES):
         span = pl.ds(n * piece, piece)
         pairs.append((mask_hbm.at[span], mask_ref.at[span]))
     for n, (src, dst) in enumerate(pairs):
         copies.append(pltpu.make_async_copy(src, dst, copy_sem.at[n]))
-    mask_copies, copies = copies[4:], copies[:4]
+    mask_copies, copies = copies[2:], copies[:2]
     tables = []
     for n, (name, top, height, left, width) in enumerate(places):
         tables.append(
@@ -302,13 +302,12 @@
                 into[n] = jnp.zeros((FREQ, 128), jnp.float32)
 
     parts_sent = spread_out([out_msg.at[n] for n in range(len(NEAR))], side, side_send, side_recv)
-    for copy in copies[:3]:
-        copy.wait()
+    copies[0].wait()
     for k in range(KERNELS):
         root = jnp.sqrt(jnp.full((1, 128), root_ref[k], jnp.float32))
         for part, ref in ((0, kr_ref), (1, ki_ref)):
             ref[k] = jnp.concatenate([kern_ref[part, k]] * 4, 1) * root
-    for copy in copies[3:] + late:
+    for copy in copies[1:] + late:
         copy.wait()
     flags = [occ_ref[at.band * slots + slot, at.column] for slot in range(slots)]
     take_in(parts_sent, side)
@@ -357,18 +356,16 @@
     arrays = all_tables(slots)
     tables, places = packed(arrays)
     dma = pltpu.SemaphoreType.DMA
-    hbm = pl.BlockSpec(memory_space=pl.ANY)
+    smem, hbm = pl.BlockSpec(memory_space=pltpu.SMEM), pl.BlockSpec(memory_space=pl.ANY)
     message = pltpu.VMEM((len(NEAR), FREQ, 128), jnp.float32)
     spectra = pltpu.VMEM((KERNELS, FREQ, 128), jnp.float32)
     return pl.pallas_call(
         lambda *refs: whole(bands, size, slots, list(arrays), places, *refs),
         out_shape=jax.ShapeDtypeStruct(((slots + 2) * 2 * FREQ, TILE), jnp.bfloat16),
-        in_specs=[hbm] * 6,
+        in_specs=[smem, smem] + [hbm] * 4,
         out_specs=VMEM,
         scratch_shapes=[pltpu.VMEM(a.shape, jnp.bfloat16) for a in arrays.values()]
         + [
-            pltpu.SMEM(weights.shape, weights.dtype),
-            pltpu.SMEM(occupancy.shape, occupancy.dtype),
             pltpu.VMEM(kernels.shape, kernels.dtype),
             pltpu.VMEM(mask_field.shape, mask_field.dtype),
             pltpu.VMEM(target_field.shape, target_field.dtype),
@@ -377,7 +374,7 @@
             message, message,
             pltpu.VMEM((FREQ, 128), jnp.float32),
             message,
-            dma((4 + PIECES,)), dma((len(places),)),
+            dma((2 + PIECES,)), dma((len(places),)),
             dma((len(NEAR),)), dma((len(NEAR),)), dma((len(NEAR),)), dma((len(NEAR),)),
         ],
         compiler_params=pltpu.CompilerParams(
@@ -392,16 +389,13 @@
     rows = 256
     steps = height // rows
 
-    def finish(table_ref, low_hbm, mask_ref, out_ref, low_ref, held, low_sem, sems):
-        fetch = pltpu.make_async_copy(low_hbm, low_ref, low_sem)
-        fetch.start()
-        values = mask_ref[...].astype(jnp.float32)
-        held[...] = GAMMA * 4.0 * values * (values * values - 1.0)
-        fetch.wait()
+    def finish(table_ref, low_ref, mask_ref, out_ref, held, sems):
         copies = []
         for step in range(steps):
             span = pl.ds(step * rows, rows)
-            held[span, :] = held[span, :] + mixed_dot(table_ref[span, :], low_ref[...])
+            values = mask_ref[span, :].astype(jnp.float32)
+            penalty = GAMMA * 4.0 * values * (values * values - 1.0)
+            held[span, :] = mixed_dot(table_ref[span, :], low_ref[...]) + penalty
             copies.append(pltpu.make_async_copy(held.at[span], out_ref.at[span], sems.at[step]))
             copies[-1].start()
         for copy in copies:
@@ -410,15 +404,10 @@
     return pl.pallas_call(
         finish,
         out_shape=jax.ShapeDtypeStruct((height, width), jnp.float32),
-        in_specs=[VMEM, pl.BlockSpec(memory_space=pl.ANY), VMEM],
+        in_specs=[VMEM, VMEM, VMEM],
         out_specs=pl.BlockSpec(memory_space=pl.ANY),
-        scratch_shapes=[
-            pltpu.VMEM(lowered.shape, lowered.dtype),
-            pltpu.VMEM((height, width), jnp.float32),
-            pltpu.SemaphoreType.DMA,
-            pltpu.SemaphoreType.DMA((steps,)),
-        ],
-        compiler_params=pltpu.CompilerParams(vmem_limit_bytes=VMEM_GRANT),
+        scratch_shapes=[pltpu.VMEM((height, width), jnp.float32), pltpu.SemaphoreType.DMA((steps,))],
+        compiler_params=pltpu.CompilerParams(vmem_limit_bytes=16 * 1024 * 1024),
     )(table, lowered, mask_field)
 
 

time: 20 us -> 19.2 us (0.960)
  Pallas kernels: 19.9 us -> 17.5 us
  local copies, waits for them, and re-layouts: 0 us -> 1.46 us
    pallas_call x1, Pallas kernels: 3.93 us -> 1.61 us  [finish_call(): pl.pallas_call(finish, out_shape=jax.ShapeDtypeStruct((height, width), jn...]
    unnamed x0 -> x8, local copies, waits for them, and re-layouts: none -> 1.46 us
where the time goes in v4:
time: 19.2 us; the launch traced here: 19 us
  Pallas kernels  17.5 us (91%)
  local copies, waits for them, and re-layouts  1.46 us (8%)
    pallas_call x1, Pallas kernels, whole_call(): pl.pallas_call(lambda *refs: whole(bands, size, slots, list(arrays), plac...  15.9 us
    pallas_call x1, Pallas kernels, finish_call(): pl.pallas_call(finish, out_shape=jax.ShapeDtypeStruct((height, width), jn...  1.61 us
    unnamed x8, local copies, waits for them, and re-layouts  1.46 us

profile of v4, /device:TPU:1, one launch (start us, length us, event | category | flops | bytes accessed | tf_op | source)
XLA Modules:
  0.0 19.0 jit_solution(15759454642725283159)
XLA Ops:
  0.0 0.0 copy-start.1
  0.0 0.0 copy-start
  0.0 0.0 copy-start.2
  0.0 0.8 %copy-done.2 = s32[8,8]{1,0:T(8,128)S(1)} copy-done((s32[8,8]{1,0:T(8,128)S(1)}, s32[8,8]{1,0:T(8,128)}, u32[]{:S(2)}) %copy-start.2) | copy-done | bytes 280
  0.8 0.0 copy-start.3
  0.8 0.7 %copy-done.3 = f32[24]{0:T(128)S(1)} copy-done((f32[24]{0:T(128)S(1)}, f32[24]{0:T(128)}, u32[]{:S(2)}) %copy-start.3) | copy-done | bytes 120
  1.5 15.9 %shard_map.73.low_ref = bf16[256,512]{1,0:T(8,128)(2,1)S(1)} custom-call(f32[24]{0:T(128)S(1)} %copy-done.3, s32[8,8]{1,0:T(8,128)S(1)} %copy-done.2, f32[2,24,32,32]{3,2,1,0:T(8,128)} %refs_2_.1, bf16[1024,512]{1,0:T(8,128)(2,1)} %mask_ref.1, bf16[1024,512]{1,0:T(8,128)(2,1)} %refs_4_.1, bf16[5504,256]{1,0:T(8,128)(2,1)} %constant.4.clone.refs_5_), custom_call_target="tpu_custom_call" | custom-call | tf_op jit(solution)/shard_map/pallas_call | solution.py:362
  17.4 0.0 copy-done.1
  17.4 0.0 copy-done
  17.4 1.6 %shard_map.74 = f32[1024,512]{1,0:T(8,128)} custom-call(bf16[1024,256]{1,0:T(8,128)(2,1)S(1)} %copy-done.1, bf16[256,512]{1,0:T(8,128)(2,1)S(1)} %shard_map.73.low_ref, bf16[1024,512]{1,0:T(8,128)(2,1)S(1)} %copy-done), custom_call_target="tpu_custom_call" | custom-call | tf_op jit(solution)/shard_map/pallas_call | solution.py:404
Async XLA Ops:
  0.0 17.4 %copy-start.1 = (bf16[1024,256]{1,0:T(8,128)(2,1)S(1)}, bf16[1024,256]{1,0:T(8,128)(2,1)}, u32[]{:S(2)}) copy-start(bf16[1024,256]{1,0:T(8,128)(2,1)} %constant.5.clone.table_ref) | copy-start | bytes 1572868
  0.0 17.4 %copy-start = (bf16[1024,512]{1,0:T(8,128)(2,1)S(1)}, bf16[1024,512]{1,0:T(8,128)(2,1)}, u32[]{:S(2)}) copy-start(bf16[1024,512]{1,0:T(8,128)(2,1)} %mask_ref.1) | copy-start | bytes 3145732
  0.0 0.8 %copy-start.2 = (s32[8,8]{1,0:T(8,128)S(1)}, s32[8,8]{1,0:T(8,128)}, u32[]{:S(2)}) copy-start(s32[8,8]{1,0:T(8,128)} %refs_1_.1) | copy-start | bytes 772
  0.8 0.7 %copy-start.3 = (f32[24]{0:T(128)S(1)}, f32[24]{0:T(128)}, u32[]{:S(2)}) copy-start(f32[24]{0:T(128)} %refs_0_.1) | copy-start | bytes 292
